TPU v7x, 256 devices: a whole 4x4x8 slice. The times are simulated.
256 devices in a mesh: band: 16 (over x, y_hi, core), strip: 16 (over y_lo, z).
Axes of the slice: x: 4, y: 4 (y_hi: 2, y_lo: 2; y = y_hi * 2 + y_lo), z: 8, core: 2. Of those that a mesh axis runs over, the one named last changes fastest.
Arguments:
- pattern: int32 [131072, 2048], P(('band', 'strip')), may hold values from 0 to 2, as said below
Outputs:
- dose: float32 [131072, 2048], P(('band', 'strip'))
- exposure: float32 [131072, 2048], P(('band', 'strip'))
Inputs may be any that keep to these rules, and one draw needn't show every extreme that they name: `pattern`: class codes: 0 clear, 1 feature interior, 2 feature edge.
All inputs are finite; a program needn't handle non-finite values.
Results may differ from a plain program's by a relative error of at most 0.0003.
Values sent between devices are 32-bit elements; how exact they have to be, the bound alone decides.
No kernel may reach another device: no remote copies, remote signals or barrier semaphores. Data moves between devices by JAX's collectives and lax.ppermute only.
A program may use at most 64 MiB of HBM per device.

v0:
```python
import functools
import math

import jax
import jax.numpy as jnp
import ml_dtypes
import numpy as np
from jax import lax
from jax.experimental import pallas as pl
from jax.experimental.pallas import tpu as pltpu
from jax.sharding import PartitionSpec as P

POOL = 256
H = 16
ETA_BACK = 0.75
SIGMA_BACK = 6.0
TOTAL = 1.0 + ETA_BACK
BACK_SHARE = ETA_BACK / TOTAL
AXES = ("band", "strip")
F32 = jnp.float32
BF16 = jnp.bfloat16
LANES = 128


def fine_taps(diff):
    spread = H / 3.0
    steps = np.arange(-H, H + 1, dtype=np.float64)
    total = np.exp(-steps * steps / (2.0 * spread * spread)).sum()
    weight = np.exp(-diff * diff / (2.0 * spread * spread)) / total
    return np.where(np.abs(diff) <= H, weight, 0.0)


def back_weight(diff, fog_sigma):
    near = np.exp(-diff * diff / (2.0 * SIGMA_BACK * SIGMA_BACK)) / (SIGMA_BACK * math.sqrt(2.0 * math.pi))
    far = np.exp(-diff * diff / (2.0 * fog_sigma * fog_sigma)) / (fog_sigma * math.sqrt(2.0 * math.pi))
    return 0.5 * near + 0.5 * far


def two_terms(matrix):
    high = matrix.astype(ml_dtypes.bfloat16)
    low = (matrix - high.astype(np.float64)).astype(ml_dtypes.bfloat16)
    return high, low


def row_taps(count, scale):
    out_rows = np.arange(count, dtype=np.float64)[:, None]
    in_rows = np.arange(count + 2 * H, dtype=np.float64)[None, :]
    return np.concatenate(two_terms(scale * fine_taps(in_rows - H - out_rows)), axis=0)


def column_taps(scale):
    ins = np.arange(POOL + 2 * LANES, dtype=np.float64)[:, None] - LANES
    outs = np.arange(POOL, dtype=np.float64)[None, :]
    return two_terms(scale * fine_taps(ins - outs))


def split(value):
    high = value.astype(BF16)
    low = (value - high.astype(F32)).astype(BF16)
    return high, low


def dot(a, b):
    return jnp.dot(a, b, preferred_element_type=F32)


def blur_down(taps, rows):
    both = dot(taps, rows)
    half = both.shape[0] // 2
    return both[:half] + both[half:]


def blur_down3(taps, high, low):
    half = taps.shape[0] // 2
    both = dot(taps, high)
    return both[:half] + both[half:] + dot(taps[:half], low)


def blur_across(high, low, taps_high, taps_low):
    return dot(high, taps_high) + dot(high, taps_low) + dot(low, taps_high)


def levels(pattern):
    return jnp.where(pattern == 1, 5.0, jnp.where(pattern == 2, 7.0, 0.0)).astype(F32)


def signed_base(pattern):
    return jnp.where(pattern == 1, 1.5, jnp.where(pattern == 2, -1.95, 0.0)).astype(F32)


def less(base, forward):
    return jnp.where(base > 0, base - forward, jnp.where(base < 0, base + forward, 0.0))


def clear_rims(ref):
    zeros = jnp.zeros((ref.shape[0], LANES), BF16)
    ref[:, :LANES] = zeros
    ref[:, ref.shape[1] - LANES :] = zeros


def span(step):
    return pl.ds(pl.multiple_of(step * POOL, POOL), POOL + 2 * LANES)


def centre(step):
    return pl.ds(pl.multiple_of(step * POOL + LANES, LANES), POOL)


def first_kernel(steps, pattern_ref, big_ref, small_ref, wh_ref, wl_ref, out_ref, sums_ref, rh, rl, base_ref):
    step = pl.program_id(0)
    rows = pattern_ref.shape[0]
    big = big_ref.shape[1]
    wide = big - 2 * H
    slot = lax.rem(step, 2)

    @pl.when(step == 0)
    def _():
        clear_rims(rh)
        clear_rims(rl)

    @pl.when(step < steps)
    def _():
        pattern = pattern_ref[...]
        level = levels(pattern)
        x = level.astype(BF16)
        base_ref[slot] = signed_base(pattern)
        parts, at = [], 0
        while at + 2 * H < rows:
            taps = big_ref[...] if at + big <= rows else small_ref[...]
            parts.append((at, blur_down(taps, x[at : at + taps.shape[1]])))
            at += wide
        for at, part in parts:
            high, low = split(part)
            rh[at : at + part.shape[0], centre(step)] = high
            rl[at : at + part.shape[0], centre(step)] = low

    @pl.when(step > 0)
    def _():
        back = step - 1
        forward = blur_across(rh[:, span(back)], rl[:, span(back)], wh_ref[...], wl_ref[...])
        base = base_ref[1 - slot]
        now = less(base[H : rows - H], forward)
        out_ref[:H] = jnp.zeros((H, POOL), F32)
        out_ref[H : rows - H] = now
        out_ref[rows - H :] = jnp.zeros((H, POOL), F32)
        size = jnp.abs(now)
        sums = []
        for first, last in ((0, POOL - H), (POOL - H, rows - 2 * H)):
            sums.append(jnp.sum(size[first:last], axis=0, keepdims=True))
        level = jnp.where(base > 0, 5.0, jnp.where(base < 0, 7.0, 0.0))
        full = jnp.where(base != 0, 1.0, 0.0)
        for value in (level, full):
            for first in (0, POOL):
                sums.append(jnp.sum(value[first : first + POOL], axis=0, keepdims=True))
        sums.append(jnp.zeros((2, POOL), F32))
        sums_ref[...] = jnp.concatenate(sums, axis=0)


def edge_kernel(cells, ends_ref, above_ref, top_ref, bottom_ref, below_ref, sums_ref, taps_ref, wh_ref, wl_ref, edge_ref, send_ref):
    width = top_ref.shape[1]
    above = jnp.where(ends_ref[0] == 0, above_ref[...], 0)
    below = jnp.where(ends_ref[1] == 0, below_ref[...], 0)
    upper = jnp.concatenate([above, top_ref[...]], axis=0)
    lower = jnp.concatenate([bottom_ref[...], below], axis=0)
    blurred = [blur_down(taps_ref[...], levels(p).astype(BF16)) for p in (upper, lower)]
    rim = jnp.zeros((4 * H, LANES), BF16)
    wide = [jnp.concatenate([rim, part, rim], axis=1) for part in split(jnp.concatenate(blurred, axis=0))]
    stacked = [
        jnp.concatenate([w[:, POOL * j : POOL * (j + 1) + 2 * LANES] for j in range(cells)], axis=0) for w in wide
    ]
    forward = blur_across(stacked[0], stacked[1], wh_ref[...], wl_ref[...])
    base = signed_base(jnp.concatenate([upper[H : 3 * H], lower[H : 3 * H]], axis=0))
    row = lax.broadcasted_iota(jnp.int32, (8, LANES), 0)
    lane = lax.broadcasted_iota(jnp.int32, (8, LANES), 1)
    spread = jnp.zeros((8, LANES), F32)
    kind = lax.broadcasted_iota(jnp.int32, (8, POOL), 0)
    for j in range(cells):
        here = slice(POOL * j, POOL * (j + 1))
        now = less(base[:, here], forward[4 * H * j : 4 * H * (j + 1)])
        edge_ref[:, here] = now
        size = jnp.abs(now)
        top = jnp.sum(size[H : 2 * H], axis=0, keepdims=True)
        bottom = jnp.sum(size[2 * H : 3 * H], axis=0, keepdims=True)
        sums = sums_ref[:, here] + jnp.where(kind == 0, top, jnp.where(kind == 1, bottom, 0.0))
        total = jnp.sum(sums, axis=1, keepdims=True)
        spread = spread + jnp.where((lane == row * cells + j), total, 0.0)
    scale = jnp.where(row < 2, 1.0, jnp.where(row < 4, 0.2, 1.0)) / (POOL * POOL)
    send_ref[...] = jnp.broadcast_to(jnp.sum(spread * scale, axis=0, keepdims=True), send_ref.shape)


def exact_dot(a, b):
    return jnp.dot(a, b, precision=lax.Precision.HIGHEST, preferred_element_type=F32)


def back_kernel(cells, me_ref, all_ref, mix_ref, kernel_ref, out_ref, b1_ref):
    me = me_ref[0]
    count = all_ref.shape[0]
    pair = 2 * cells
    got = all_ref[...]
    adjusted = pltpu.roll(got, 0, 1)
    coarse = pltpu.roll(got, LANES - pair, 1)
    full = pltpu.roll(got, LANES - 2 * pair, 1)

    def mixed(value):
        three = exact_dot(value, mix_ref[...])
        return jnp.concatenate([three[:, LANES * i : LANES * (i + 1)] for i in range(3)], axis=0)

    b1 = exact_dot(kernel_ref[...], mixed(coarse))
    b1_ref[...] = b1
    second = adjusted - BACK_SHARE * b1 * full
    mine = jnp.broadcast_to(kernel_ref[pl.ds(me, 1), :], (8, 3 * count))
    b2 = exact_dot(mine, mixed(second))
    before = b1_ref[pl.ds(jnp.maximum(me - 1, 0), 1), :]
    here = b1_ref[pl.ds(me, 1), :]
    after = b1_ref[pl.ds(jnp.minimum(me + 1, count - 1), 1), :]
    own = b2[:1]
    lines = ((before, 1), (here, 0), (here, 1), (after, 0), (own, 0), (own, 1))
    for at, (value, half) in enumerate(lines):
        for j in range(cells):
            lane = half * cells + j
            out_ref[at : at + 1, POOL * j : POOL * (j + 1)] = jnp.broadcast_to(
                BACK_SHARE * value[:, lane : lane + 1], (1, POOL)
            )
    out_ref[6:8] = jnp.zeros((2, out_ref.shape[1]), F32)


def second_kernel(steps, now_ref, edge_ref, back_ref, last_ref, big_ref, small_ref, wh_ref, wl_ref, dose_ref, exposure_ref, rh, rl, base_ref):
    step = pl.program_id(0)
    rows = now_ref.shape[0]
    big = big_ref.shape[1]
    wide = big - 2 * H
    slot = lax.rem(step, 2)

    @pl.when(step == 0)
    def _():
        clear_rims(rh)
        clear_rims(rl)

    @pl.when(step < steps)
    def _():
        edge = edge_ref[...]
        pieces = [
            (edge[:H], 0),
            (edge[H : 2 * H], 1),
            (now_ref[H:POOL], 1),
            (now_ref[POOL : rows - H], 2),
            (edge[2 * H : 3 * H], 2),
            (edge[3 * H :], 3),
        ]
        doses, bases = [], []
        for value, line in pieces:
            level = jnp.where(value != 0, jnp.abs(value) - back_ref[line : line + 1], 0.0)
            doses.append(level)
            bases.append(jnp.where(value > 0, level + 0.5, jnp.where(value < 0, level + 0.55, 0.0)))
        base_ref[slot] = jnp.concatenate(bases[1:5], axis=0)
        high, low = split(jnp.concatenate(doses, axis=0))
        at = 0
        while at < rows:
            taps = big_ref[...] if at + big <= rows + 2 * H else small_ref[...]
            depth = taps.shape[1]
            part = blur_down3(taps, high[at : at + depth], low[at : at + depth])
            part_high, part_low = split(part)
            rh[at : at + part.shape[0], centre(step)] = part_high
            rl[at : at + part.shape[0], centre(step)] = part_low
            at += wide

    @pl.when(step > 0)
    def _():
        back = step - 1
        forward = blur_across(rh[:, span(back)], rl[:, span(back)], wh_ref[...], wl_ref[...])
        base = base_ref[1 - slot]
        own = jnp.concatenate(
            [jnp.broadcast_to(last_ref[4:5], (POOL, POOL)), jnp.broadcast_to(last_ref[5:6], (rows - POOL, POOL))], axis=0
        )
        exposure = forward + own
        exposure_ref[...] = exposure
        dose_ref[...] = jnp.where(base > 0, base - exposure, 0.0)


def whole(shape):
    return pl.BlockSpec(shape, lambda *_: (0,) * len(shape))


def local(pattern):
    rows, width = pattern.shape
    cells = width // POOL
    coarse_rows = rows // POOL
    count = lax.axis_size(AXES)
    me = lax.axis_index(AXES)
    fog_sigma = coarse_rows * count / 4.0
    wide = POOL - 2 * H
    params = functools.partial(pltpu.CompilerParams, vmem_limit_bytes=56 * 2**20)

    forward_ring = [(i, (i + 1) % count) for i in range(count)]
    backward_ring = [(j, i) for i, j in forward_ring]
    above = lax.ppermute(pattern[rows - 2 * H :], AXES, forward_ring)
    below = lax.ppermute(pattern[: 2 * H], AXES, backward_ring)

    taps_high, taps_low = (jnp.asarray(m) for m in column_taps(1.0 / TOTAL))
    column_spec = [whole(taps_high.shape)] * 2
    padded = width + 2 * LANES

    def at_step(step):
        return (0, jnp.minimum(step, cells - 1))

    def behind(step):
        return (0, jnp.maximum(step - 1, 0))

    big = jnp.asarray(row_taps(wide, 0.2))
    rest = (rows - 2 * H) % wide
    small = jnp.asarray(row_taps(rest, 0.2))
    now, sums = pl.pallas_call(
        functools.partial(first_kernel, cells),
        grid=(cells + 1,),
        in_specs=[pl.BlockSpec((rows, POOL), at_step), whole(big.shape), whole(small.shape)] + column_spec,
        out_specs=[pl.BlockSpec((rows, POOL), behind), pl.BlockSpec((8, POOL), behind)],
        out_shape=[jax.ShapeDtypeStruct((rows, width), F32), jax.ShapeDtypeStruct((8, width), F32)],
        scratch_shapes=[
            pltpu.VMEM((rows - 2 * H, padded), BF16),
            pltpu.VMEM((rows - 2 * H, padded), BF16),
            pltpu.VMEM((2, rows, POOL), F32),
        ],
        compiler_params=params(),
        cost_estimate=pl.CostEstimate(flops=6 * 10**9, bytes_accessed=3 * 10**7, transcendentals=0),
        name="first_blur",
    )(pattern, big, small, taps_high, taps_low)

    ends = jnp.stack([me == 0, me == count - 1]).astype(jnp.int32)
    edge_taps = jnp.asarray(row_taps(2 * H, 0.2))
    strip = (2 * H, width)
    last_block = rows // (2 * H) - 1
    edge, send = pl.pallas_call(
        functools.partial(edge_kernel, cells),
        grid=(1,),
        in_specs=[
            pl.BlockSpec(memory_space=pltpu.SMEM),
            whole(strip),
            whole(strip),
            pl.BlockSpec(strip, lambda i: (last_block, 0)),
            whole(strip),
            whole((8, width)),
            whole(edge_taps.shape),
        ]
        + column_spec,
        out_specs=[whole((4 * H, width)), whole((count, LANES))],
        out_shape=[jax.ShapeDtypeStruct((4 * H, width), F32), jax.ShapeDtypeStruct((count, LANES), F32)],
        compiler_params=params(),
        name="edge_blur",
    )(ends, above, pattern, pattern, below, sums, edge_taps, taps_high, taps_low)

    gathered = lax.all_to_all(send.reshape(count, 1, LANES), AXES, 0, 0, tiled=True).reshape(count, LANES)

    cols = np.arange(cells, dtype=np.float64)
    across = back_weight(cols[:, None] - cols[None, :], fog_sigma)
    mix = np.zeros((LANES, 3 * LANES))
    for half in range(2):
        mine = slice(half * cells, (half + 1) * cells)
        other = slice((1 - half) * cells, (2 - half) * cells)
        mix[mine, mine] = across
        where = LANES if half == 1 else 2 * LANES
        mix[mine, where + other.start : where + other.stop] = across
    strips = np.arange(count, dtype=np.float64)
    gap = 2.0 * (strips[None, :] - strips[:, None])
    down = np.concatenate([back_weight(gap + shift, fog_sigma) for shift in (0.0, 1.0, -1.0)], axis=1)
    back = pl.pallas_call(
        functools.partial(back_kernel, cells),
        grid=(1,),
        in_specs=[
            pl.BlockSpec(memory_space=pltpu.SMEM),
            whole((count, LANES)),
            whole(mix.shape),
            whole(down.shape),
        ],
        out_specs=whole((8, width)),
        out_shape=jax.ShapeDtypeStruct((8, width), F32),
        scratch_shapes=[pltpu.VMEM((count, LANES), F32)],
        compiler_params=params(),
        name="backscatter",
    )(me[None].astype(jnp.int32), gathered, jnp.asarray(mix.astype(np.float32)), jnp.asarray(down.astype(np.float32)))

    big = jnp.asarray(row_taps(wide, 1.0))
    rest = rows % wide
    small = jnp.asarray(row_taps(rest, 1.0))
    return pl.pallas_call(
        functools.partial(second_kernel, cells),
        grid=(cells + 1,),
        in_specs=[
            pl.BlockSpec((rows, POOL), at_step),
            pl.BlockSpec((4 * H, POOL), at_step),
            pl.BlockSpec((8, POOL), at_step),
            pl.BlockSpec((8, POOL), behind),
            whole(big.shape),
            whole(small.shape),
        ]
        + column_spec,
        out_specs=[pl.BlockSpec((rows, POOL), behind)] * 2,
        out_shape=[jax.ShapeDtypeStruct((rows, width), F32)] * 2,
        scratch_shapes=[
            pltpu.VMEM((rows, padded), BF16),
            pltpu.VMEM((rows, padded), BF16),
            pltpu.VMEM((2, rows, POOL), F32),
        ],
        compiler_params=params(),
        cost_estimate=pl.CostEstimate(flops=8 * 10**9, bytes_accessed=3 * 10**7, transcendentals=0),
        name="second_blur",
    )(now, edge, back, back, big, small, taps_high, taps_low)


def solution(mesh):
    return jax.shard_map(
        local,
        mesh=mesh,
        in_specs=(P(AXES, None),),
        out_specs=(P(AXES, None), P(AXES, None)),
        check_vma=False,
    )
```

profile of v0, /device:TPU:1, one launch (start us, length us, event | category | flops | bytes accessed | tf_op | source)
XLA Modules:
  0.0 68.5 jit_solution(6848622790441505058)
XLA Ops:
  0.6 1.1 %fusion = (s32[32,2048]{1,0:T(8,128)S(1)}, s32[32,2048]{1,0:T(8,128)S(1)}) fusion(s32[512,2048]{1,0:T(8,128)} %bottom_ref.1), kind=kLoop, calls=%fused_computation.1 | loop fusion | bytes 1048576 | tf_op jit(solution)/shard_map/slice | solution.py:297
  1.7 8.1 %collective-permute-start.1 = (s32[32,2048]{1,0:T(8,128)S(1)}, s32[32,2048]{1,0:T(8,128)S(1)}, u32[]{:S(2)}, u32[]{:S(2)}) collective-permute-start(s32[32,2048]{1,0:T(8,128)S(1)} %get-tuple-element.10), channel_id=1, source_target_pairs={{1,0},{2,1},{3,2},{4,3},{5,4},{6,5},{7,6},{8,7},{9,8},{10,9},{11,1... | collective-permute-start | bytes 786440 | tf_op jit(solution)/shard_map/ppermute | solution.py:297
  9.8 0.0 collective-permute-start
  9.8 11.1 %first_blur.1 = (f32[512,2048]{1,0:T(8,128)}, f32[8,2048]{1,0:T(8,128)}) custom-call(s32[512,2048]{1,0:T(8,128)} %bottom_ref.1, bf16[448,256]{1,0:T(8,128)(2,1)} %constant.31.clone.big_ref, bf16[64,64]{1,0:T(8,128)(2,1)} %constant.32.clone.small_ref.taps_ref, bf16[512,256]{1,0:T(8,128)(2,1)} %constant.29.clone.wh_ref, bf16[512,256]{1,0:T(8,128)(2,1)} %constant.30.clone.wl_ref), custom_call_target="tpu_custom_call" | custom-call | flops 6000000000 | bytes 30000000 | tf_op jit(solution)/shard_map/first_blur/pallas_call | solution.py:312
  20.9 0.6 add_convert_fusion.ends_ref
  21.5 0.0 collective-permute-done.1.below_ref
  21.5 0.0 copy-start
  21.5 0.0 collective-permute-done.above_ref
  21.5 0.0 copy-start.1
  21.5 0.7 copy-done
  22.2 0.1 copy-done.1
  22.3 3.1 %edge_blur.1 = (f32[64,2048]{1,0:T(8,128)}, f32[256,128]{1,0:T(8,128)}) custom-call(s32[2]{0:T(128)} %add_convert_fusion.ends_ref, s32[32,2048]{1,0:T(8,128)} %copy-done.1, s32[512,2048]{1,0:T(8,128)} %bottom_ref.1, s32[512,2048]{1,0:T(8,128)} %bottom_ref.1, s32[32,2048]{1,0:T(8,128)} %copy-done, f32[8,2048]{1,0:T(8,128)} %get-tuple-element.7.sums_ref, ...), custom_call_target="tpu_custom_call" | custom-call | tf_op jit(solution)/shard_map/edge_blur/pallas_call | solution.py:332
  25.3 25.8 %all_to_all.5 = f32[256,1,128]{2,1,0:T(1,128)} all-to-all(f32[256,1,128]{2,1,0:T(1,128)} %bitcast.8), channel_id=1, replica_groups=mesh['band'=16,'strip'=16] {'band','strip'}, dimensions={0} | all-to-all | bytes 262144 | tf_op jit(solution)/shard_map/all_to_all | solution.py:351
  51.2 4.9 %backscatter.1.back_ref.last_ref = f32[8,2048]{1,0:T(8,128)} custom-call(s32[1]{0:T(128)} %bitcast.2.me_ref, f32[256,128]{1,0:T(8,128)} %bitcast.7, f32[128,384]{1,0:T(8,128)} %constant.33.clone.mix_ref, f32[256,768]{1,0:T(8,128)} %constant.34.clone.kernel_ref), custom_call_target="tpu_custom_call" | custom-call | tf_op jit(solution)/shard_map/backscatter/pallas_call | solution.py:365
  56.0 12.5 %second_blur.1 = (f32[512,2048]{1,0:T(8,128)}, f32[512,2048]{1,0:T(8,128)}) custom-call(f32[512,2048]{1,0:T(8,128)} %get-tuple-element.6.now_ref, f32[64,2048]{1,0:T(8,128)} %get-tuple-element.8.edge_ref, f32[8,2048]{1,0:T(8,128)} %backscatter.1.back_ref.last_ref, f32[8,2048]{1,0:T(8,128)} %backscatter.1.back_ref.last_ref, ...), custom_call_target="tpu_custom_call" | custom-call | flops 8000000000 | bytes 30000000 | tf_op jit(solution)/shard_map/second_blur/pallas_call | solution.py:384
Async XLA Ops:
  1.7 19.8 %collective-permute-start.1 = (s32[32,2048]{1,0:T(8,128)S(1)}, s32[32,2048]{1,0:T(8,128)S(1)}, u32[]{:S(2)}, u32[]{:S(2)}) collective-permute-start(s32[32,2048]{1,0:T(8,128)S(1)} %get-tuple-element.10), channel_id=1, source_target_pairs={{1,0},{2,1},{3,2},{4,3},{5,4},{6,5},{7,6},{8,7},{9,8},{10,9},{11,1... | collective-permute-start | bytes 786440 | tf_op jit(solution)/shard_map/ppermute | solution.py:297
  9.8 11.7 %collective-permute-start = (s32[32,2048]{1,0:T(8,128)S(1)}, s32[32,2048]{1,0:T(8,128)S(1)}, u32[]{:S(2)}, u32[]{:S(2)}) collective-permute-start(s32[32,2048]{1,0:T(8,128)S(1)} %get-tuple-element.11), channel_id=1, source_target_pairs={{0,1},{1,2},{2,3},{3,4},{4,5},{5,6},{6,7},{7,8},{8,9},{9,10},{10,1... | collective-permute-start | bytes 786440 | tf_op jit(solution)/shard_map/ppermute | solution.py:296
  21.5 0.7 %copy-start = (s32[32,2048]{1,0:T(8,128)}, s32[32,2048]{1,0:T(8,128)S(1)}, u32[]{:S(2)}) copy-start(s32[32,2048]{1,0:T(8,128)S(1)} %collective-permute-done.1.below_ref) | copy-start | bytes 786436
  21.5 0.8 %copy-start.1 = (s32[32,2048]{1,0:T(8,128)}, s32[32,2048]{1,0:T(8,128)S(1)}, u32[]{:S(2)}) copy-start(s32[32,2048]{1,0:T(8,128)S(1)} %collective-permute-done.above_ref) | copy-start | bytes 786436
where the time goes:
time: 69.1 us; the launch traced here: 68.5 us
  Pallas kernels  31.5 us (46%)
  blocking collectives  25.8 us (37%)
  starting transfers between devices  8.06 us (12%)
  local copies, waits for them, and re-layouts  1.84 us (3%)
    all_to_all x1, blocking collectives, local(): lax.all_to_all(send.reshape(count, 1, LANES), AXES, 0, 0, tiled=True)  25.8 us
    pallas_call x1, Pallas kernels, local(): pl.pallas_call(functools.partial(second_kernel, cells), grid=(cells + 1,)...  12.5 us
    pallas_call x1, Pallas kernels, local(): pl.pallas_call(functools.partial(first_kernel, cells), grid=(cells + 1,),...  11.1 us
    ppermute x1, starting transfers between devices, local(): below = lax.ppermute(pattern[:2 * H], AXES, backward_ring)  8.06 us
    pallas_call x1, Pallas kernels, local(): pl.pallas_call(functools.partial(back_kernel, cells), grid=(1,), in_specs...  4.87 us
    pallas_call x1, Pallas kernels, local(): pl.pallas_call(functools.partial(edge_kernel, cells), grid=(1,), in_specs...  3.09 us
  transfers between devices with their start and end apart: 2, of which 0 were waited for; matrix products, arithmetic and copies ran while one was open for 1% of the time, Pallas kernels for 16%

commit v1 on v0

v1 whole, which is shorter than its diff:
```python
import functools
import math

import jax
import jax.numpy as jnp
import ml_dtypes
import numpy as np
from jax import lax
from jax.experimental import pallas as pl
from jax.experimental.pallas import tpu as pltpu
from jax.sharding import PartitionSpec as P

POOL = 256
H = 16
ETA_BACK = 0.75
SIGMA_BACK = 6.0
TOTAL = 1.0 + ETA_BACK
BACK_SHARE = ETA_BACK / TOTAL
AXES = ("band", "strip")
F32 = jnp.float32
BF16 = jnp.bfloat16
LANES = 128


def fine_taps(diff):
    spread = H / 3.0
    steps = np.arange(-H, H + 1, dtype=np.float64)
    total = np.exp(-steps * steps / (2.0 * spread * spread)).sum()
    weight = np.exp(-diff * diff / (2.0 * spread * spread)) / total
    return np.where(np.abs(diff) <= H, weight, 0.0)


def back_weight(diff, fog_sigma):
    near = np.exp(-diff * diff / (2.0 * SIGMA_BACK * SIGMA_BACK)) / (SIGMA_BACK * math.sqrt(2.0 * math.pi))
    far = np.exp(-diff * diff / (2.0 * fog_sigma * fog_sigma)) / (fog_sigma * math.sqrt(2.0 * math.pi))
    return 0.5 * near + 0.5 * far


def two_terms(matrix):
    high = matrix.astype(ml_dtypes.bfloat16)
    low = (matrix - high.astype(np.float64)).astype(ml_dtypes.bfloat16)
    return high, low


def row_taps(count, scale):
    out_rows = np.arange(count, dtype=np.float64)[:, None]
    in_rows = np.arange(count + 2 * H, dtype=np.float64)[None, :]
    return np.concatenate(two_terms(scale * fine_taps(in_rows - H - out_rows)), axis=0)


def column_taps(scale):
    ins = np.arange(POOL + 2 * LANES, dtype=np.float64)[:, None] - LANES
    outs = np.arange(POOL, dtype=np.float64)[None, :]
    return two_terms(scale * fine_taps(ins - outs))


def split(value):
    high = value.astype(BF16)
    low = (value - high.astype(F32)).astype(BF16)
    return high, low


def dot(a, b):
    return jnp.dot(a, b, preferred_element_type=F32)


def blur_down(taps, rows):
    both = dot(taps, rows)
    half = both.shape[0] // 2
    return both[:half] + both[half:]


def blur_down3(taps, high, low):
    half = taps.shape[0] // 2
    both = dot(taps, high)
    return both[:half] + both[half:] + dot(taps[:half], low)


def blur_across(high, low, taps_high, taps_low):
    return dot(high, taps_high) + dot(high, taps_low) + dot(low, taps_high)


def clear_rims(ref):
    zeros = jnp.zeros((ref.shape[0], LANES), BF16)
    ref[:, :LANES] = zeros
    ref[:, ref.shape[1] - LANES :] = zeros


def pixels(pattern):
    kind = pattern.astype(F32)
    return kind, jnp.where(pattern == 2, 7.0, 5.0 * kind)


LIFT = 1.05
MIDDLE = 1.85


def column_sums(value):
    return jnp.sum(value, axis=0, keepdims=True)


def rims_kernel(pattern_hbm, odd_ref, even_ref, sem):
    rows, rim = pattern_hbm.shape[0], odd_ref.shape[0]
    last = rows - rim
    odd = lax.rem(lax.axis_index(AXES), 2)
    copies = [
        pltpu.make_async_copy(pattern_hbm.at[pl.ds(pl.multiple_of(start, rim), rim)], ref, sem.at[i])
        for i, (ref, start) in enumerate(((odd_ref, odd * last), (even_ref, (1 - odd) * last)))
    ]
    for copy in copies:
        copy.start()
    for copy in copies:
        copy.wait()


def first_kernel(
    pattern_hbm, big_hbm, small_hbm, wh_hbm, wl_hbm, out_hbm, sums_ref,
    pattern_ref, out_ref, big_ref, small_ref, wh_ref, wl_ref, rh, rl, in_sem, out_sem, taps_sem,
):
    rows, width = pattern_ref.shape
    cells = width // POOL
    big = big_ref.shape[1]
    wide = big - 2 * H

    def cell(t):
        return slice(POOL * t, POOL * (t + 1))

    loads = [pltpu.make_async_copy(pattern_hbm.at[:, cell(t)], pattern_ref.at[:, cell(t)], in_sem.at[t]) for t in range(cells)]
    stores = [pltpu.make_async_copy(out_ref.at[:, cell(t)], out_hbm.at[:, cell(t)], out_sem.at[t]) for t in range(cells)]
    pairs = ((big_hbm, big_ref), (small_hbm, small_ref), (wh_hbm, wh_ref), (wl_hbm, wl_ref))
    taps_loads = [pltpu.make_async_copy(hbm, ref, taps_sem.at[i]) for i, (hbm, ref) in enumerate(pairs)]
    for load in loads[:1] + taps_loads + loads[1:]:
        load.start()
    clear_rims(rh)
    clear_rims(rl)
    for load in taps_loads:
        load.wait()

    def down(t):
        here = slice(POOL * t + LANES, POOL * (t + 1) + LANES)
        _, level = pixels(pattern_ref[:, cell(t)])
        x = level.astype(BF16)
        at = 0
        while at + 2 * H < rows:
            taps = big_ref[...] if at + big <= rows else small_ref[...]
            part = blur_down(taps, x[at : at + taps.shape[1]])
            rh[at : at + part.shape[0], here], rl[at : at + part.shape[0], here] = split(part)
            at += wide

    def across(t):
        window = slice(POOL * t, POOL * (t + 1) + 2 * LANES)
        forward = blur_across(rh[:, window], rl[:, window], wh_ref[...], wl_ref[...])
        kind, level = pixels(pattern_ref[:, cell(t)])
        now = jnp.maximum(1.5 * kind[H : rows - H] - forward, 0.0)
        zeros = jnp.zeros((H, POOL), F32)
        out_ref[:H, cell(t)] = zeros
        out_ref[H : rows - H, cell(t)] = now
        out_ref[rows - H :, cell(t)] = zeros
        sums = [column_sums(now[: POOL - H]), column_sums(now[POOL - H :])]
        sums += [column_sums(value[first : first + POOL]) for value in (level, kind) for first in (0, POOL)]
        sums_ref[:, cell(t)] = jnp.concatenate(sums + [jnp.zeros((2, POOL), F32)], axis=0)
        stores[t].start()

    for t in range(cells + 1):
        if t < cells:
            loads[t].wait()
            down(t)
        if t > 0:
            across(t - 1)
    for store in stores:
        store.wait()


def edge_kernel(for_odd_ref, for_even_ref, from_odd_ref, from_even_ref, sums_ref, taps_ref, wh_ref, wl_ref, edge_ref, send_ref):
    count = lax.axis_size(AXES)
    me = lax.axis_index(AXES)
    width = edge_ref.shape[1]
    cells = width // POOL
    even = lax.rem(me, 2) == 0
    top = jnp.where(even, for_odd_ref[...], for_even_ref[...])
    bottom = jnp.where(even, for_even_ref[...], for_odd_ref[...])
    above = jnp.where(even, from_odd_ref[...], from_even_ref[...])
    below = jnp.where(even, from_even_ref[...], from_odd_ref[...])
    above = jnp.where(me > 0, above, 0)
    below = jnp.where(me < count - 1, below, 0)
    upper = jnp.concatenate([above, top], axis=0)
    lower = jnp.concatenate([bottom, below], axis=0)
    blurred = [blur_down(taps_ref[...], pixels(p)[1].astype(BF16)) for p in (upper, lower)]
    rim = jnp.zeros((4 * H, LANES), BF16)
    wide = [jnp.concatenate([rim, part, rim], axis=1) for part in split(jnp.concatenate(blurred, axis=0))]
    stacked = [
        jnp.concatenate([w[:, POOL * j : POOL * (j + 1) + 2 * LANES] for j in range(cells)], axis=0) for w in wide
    ]
    forward = blur_across(stacked[0], stacked[1], wh_ref[...], wl_ref[...])
    kind = jnp.concatenate([upper[H : 3 * H], lower[H : 3 * H]], axis=0).astype(F32)
    row = lax.broadcasted_iota(jnp.int32, (8, POOL), 0)
    place = lax.broadcasted_iota(jnp.int32, (8, LANES), 0)
    lane = lax.broadcasted_iota(jnp.int32, (8, LANES), 1)
    spread = jnp.zeros((8, LANES), F32)
    for j in range(cells):
        here = slice(POOL * j, POOL * (j + 1))
        now = jnp.maximum(1.5 * kind[:, here] - forward[4 * H * j : 4 * H * (j + 1)], 0.0)
        edge_ref[:, here] = now
        top, bottom = column_sums(now[H : 2 * H]), column_sums(now[2 * H : 3 * H])
        sums = sums_ref[:, here] + jnp.where(row == 0, top, jnp.where(row == 1, bottom, 0.0))
        total = jnp.sum(sums, axis=1, keepdims=True)
        value, fifths, classes = total[0:2], total[2:4], total[4:6]
        second = (5.0 * classes - fifths) * (1.0 / 3.0)
        total = jnp.concatenate([value - LIFT * second, 0.2 * fifths, classes - second, jnp.zeros((2, 1), F32)], axis=0)
        spread = spread + jnp.where(lane == place * cells + j, total, 0.0)
    line = column_sums(spread) * (1.0 / (POOL * POOL))
    send_ref[...] = jnp.broadcast_to(line, send_ref.shape)


def product(a, b):
    return dot(a[0], b[0]) + dot(a[1], b[0]) + dot(a[0], b[1])


def find_back(me, all_ref, mix, kernel, up_ref, b1_ref, b2_ref):
    count = all_ref.shape[0]
    cells = up_ref.shape[1] // POOL
    pair = 2 * cells
    adjusted = all_ref[...]
    coarse = pltpu.roll(adjusted, LANES - pair, 1)
    full = pltpu.roll(adjusted, LANES - 2 * pair, 1)

    def scatter(value):
        three = product(split(value), mix)
        return product(kernel, split(jnp.concatenate([three[:, LANES * i : LANES * (i + 1)] for i in range(3)], axis=0)))

    b1 = scatter(coarse)
    b1_ref[...] = b1
    b2_ref[...] = scatter(adjusted - BACK_SHARE * b1 * full)
    before = b1_ref[pl.ds(jnp.maximum(me - 1, 0), 1), :]
    here = b1_ref[pl.ds(me, 1), :]
    after = b1_ref[pl.ds(jnp.minimum(me + 1, count - 1), 1), :]
    own = b2_ref[pl.ds(me, 1), :]
    for at, (value, half) in enumerate(((before, 1), (here, 0), (here, 1), (after, 0), (own, 0), (own, 1))):
        value = BACK_SHARE * value
        for j in range(cells):
            lane = half * cells + j
            up_ref[at : at + 1, POOL * j : POOL * (j + 1)] = jnp.broadcast_to(value[:, lane : lane + 1], (1, POOL))


def second_kernel(
    now_hbm, edge_ref, all_ref, mixh_ref, mixl_ref, kerh_ref, kerl_ref, big_ref, small_ref, wh_ref, wl_ref,
    dose_hbm, exposure_hbm,
    now_ref, dose_ref, exposure_ref, rh, rl, up_ref, b1_ref, b2_ref, in_sem, dose_sem, exposure_sem,
):
    rows, width = now_ref.shape
    cells = width // POOL
    big = big_ref.shape[1]
    wide = big - 2 * H

    def cell(t):
        return slice(POOL * t, POOL * (t + 1))

    loads = [pltpu.make_async_copy(now_hbm.at[:, cell(t)], now_ref.at[:, cell(t)], in_sem.at[t]) for t in range(cells)]
    stores = [
        [pltpu.make_async_copy(ref.at[:, cell(t)], hbm.at[:, cell(t)], sem.at[t]) for t in range(cells)]
        for ref, hbm, sem in ((dose_ref, dose_hbm, dose_sem), (exposure_ref, exposure_hbm, exposure_sem))
    ]
    for load in loads:
        load.start()
    clear_rims(rh)
    clear_rims(rl)
    find_back(
        lax.axis_index(AXES), all_ref, (mixh_ref[...], mixl_ref[...]), (kerh_ref[...], kerl_ref[...]), up_ref, b1_ref, b2_ref
    )

    def down(t):
        here = slice(POOL * t + LANES, POOL * (t + 1) + LANES)
        edge = edge_ref[:, cell(t)]
        pieces = [
            (edge[:H], 0),
            (edge[H : 2 * H], 1),
            (now_ref[H:POOL, cell(t)], 1),
            (now_ref[POOL : rows - H, cell(t)], 2),
            (edge[2 * H : 3 * H], 2),
            (edge[3 * H :], 3),
        ]
        doses, at = [], -H
        for value, line in pieces:
            second = value > MIDDLE
            dose = value - up_ref[line : line + 1, cell(t)]
            dose = jnp.maximum(jnp.where(second, dose - LIFT, dose), 0.0)
            doses.append(dose)
            if 0 <= at < rows:
                base = jnp.where(dose > 0, dose + jnp.where(second, 0.55, 0.5), 0.0)
                dose_ref[at : at + value.shape[0], cell(t)] = base
            at += value.shape[0]
        high, low = split(jnp.concatenate(doses, axis=0))
        at = 0
        while at < rows:
            taps = big_ref[...] if at + big <= rows + 2 * H else small_ref[...]
            depth = taps.shape[1]
            part = blur_down3(taps, high[at : at + depth], low[at : at + depth])
            rh[at : at + part.shape[0], here], rl[at : at + part.shape[0], here] = split(part)
            at += wide

    def across(t):
        window = slice(POOL * t, POOL * (t + 1) + 2 * LANES)
        forward = blur_across(rh[:, window], rl[:, window], wh_ref[...], wl_ref[...])
        for half in range(rows // POOL):
            these = slice(POOL * half, POOL * (half + 1))
            exposure = forward[these] + up_ref[4 + half : 5 + half, cell(t)]
            base = dose_ref[these, cell(t)]
            exposure_ref[these, cell(t)] = exposure
            dose_ref[these, cell(t)] = jnp.where(base > 0, base - exposure, 0.0)
        for group in stores:
            group[t].start()

    for t in range(cells + 1):
        if t < cells:
            loads[t].wait()
            down(t)
        if t > 0:
            across(t - 1)
    for group in stores:
        for store in group:
            store.wait()


VMEM = pl.BlockSpec(memory_space=pltpu.VMEM)
HBM = pl.BlockSpec(memory_space=pltpu.HBM)


def local(pattern):
    rows, width = pattern.shape
    cells = width // POOL
    coarse_rows = rows // POOL
    count = lax.axis_size(AXES)
    fog_sigma = coarse_rows * count / 4.0
    wide = POOL - 2 * H
    padded = width + 2 * LANES
    def params(mebibytes):
        return pltpu.CompilerParams(vmem_limit_bytes=mebibytes * 2**20)

    odd_pairs = [(i, i if i in (0, count - 1) else ((i + 1) ^ 1) - 1) for i in range(count)]
    even_pairs = [(i, i ^ 1) for i in range(count)]
    for_odd, for_even = pl.pallas_call(
        rims_kernel,
        in_specs=[HBM],
        out_specs=[VMEM] * 2,
        out_shape=[jax.ShapeDtypeStruct((2 * H, width), pattern.dtype)] * 2,
        scratch_shapes=[pltpu.SemaphoreType.DMA((2,))],
        name="rims",
    )(pattern)
    from_odd = lax.ppermute(for_odd, AXES, odd_pairs)
    from_even = lax.ppermute(for_even, AXES, even_pairs)

    taps_high, taps_low = (jnp.asarray(m) for m in column_taps(1.0 / TOTAL))

    big = jnp.asarray(row_taps(wide, 0.2))
    small = jnp.asarray(row_taps((rows - 2 * H) % wide, 0.2))
    now, sums = pl.pallas_call(
        first_kernel,
        in_specs=[HBM] * 5,
        out_specs=[HBM, VMEM],
        out_shape=[jax.ShapeDtypeStruct((rows, width), F32), jax.ShapeDtypeStruct((8, width), F32)],
        scratch_shapes=[pltpu.VMEM((rows, width), jnp.int32), pltpu.VMEM((rows, width), F32)]
        + [pltpu.VMEM(m.shape, BF16) for m in (big, small, taps_high, taps_low)]
        + [pltpu.VMEM((rows - 2 * H, padded), BF16)] * 2
        + [pltpu.SemaphoreType.DMA((cells,))] * 2
        + [pltpu.SemaphoreType.DMA((4,))],
        compiler_params=params(52),
        cost_estimate=pl.CostEstimate(flops=6 * 10**9, bytes_accessed=3 * 10**7, transcendentals=0),
        name="first_blur",
    )(pattern, big, small, taps_high, taps_low)

    edge_taps = jnp.asarray(row_taps(2 * H, 0.2))
    edge, send = pl.pallas_call(
        edge_kernel,
        in_specs=[VMEM] * 8,
        out_specs=[VMEM] * 2,
        out_shape=[jax.ShapeDtypeStruct((4 * H, width), F32), jax.ShapeDtypeStruct((count, LANES), F32)],
        compiler_params=params(40),
        name="edge_blur",
    )(for_odd, for_even, from_odd, from_even, sums, edge_taps, taps_high, taps_low)

    gathered = lax.all_to_all(send.reshape(count, 1, LANES), AXES, 0, 0, tiled=True).reshape(count, LANES)

    cols = np.arange(cells, dtype=np.float64)
    across = back_weight(cols[:, None] - cols[None, :], fog_sigma)
    mix = np.zeros((LANES, 3 * LANES))
    for half in range(2):
        mine = slice(half * cells, (half + 1) * cells)
        other = slice((1 - half) * cells, (2 - half) * cells)
        mix[mine, mine] = across
        where = LANES if half == 1 else 2 * LANES
        mix[mine, where + other.start : where + other.stop] = across
    strips = np.arange(count, dtype=np.float64)
    gap = 2.0 * (strips[None, :] - strips[:, None])
    down = np.concatenate([back_weight(gap + shift, fog_sigma) for shift in (0.0, 1.0, -1.0)], axis=1)
    constants = [jnp.asarray(m) for m in two_terms(mix) + two_terms(down)]

    big = jnp.asarray(row_taps(wide, 1.0))
    small = jnp.asarray(row_taps(rows % wide, 1.0))
    return pl.pallas_call(
        second_kernel,
        in_specs=[HBM] + [VMEM] * 10,
        out_specs=[HBM] * 2,
        out_shape=[jax.ShapeDtypeStruct((rows, width), F32)] * 2,
        scratch_shapes=[pltpu.VMEM((rows, width), F32)] * 3
        + [pltpu.VMEM((rows, padded), BF16)] * 2
        + [pltpu.VMEM((8, width), F32)]
        + [pltpu.VMEM((count, LANES), F32)] * 2
        + [pltpu.SemaphoreType.DMA((cells,))] * 3,
        compiler_params=params(50),
        cost_estimate=pl.CostEstimate(flops=8 * 10**9, bytes_accessed=3 * 10**7, transcendentals=0),
        name="second_blur",
    )(now, edge, gathered, *constants, big, small, taps_high, taps_low)


def solution(mesh):
    return jax.shard_map(
        local,
        mesh=mesh,
        in_specs=(P(AXES, None),),
        out_specs=(P(AXES, None), P(AXES, None)),
        check_vma=False,
    )
```

time: 69.1 us -> 62.4 us (0.903)
  blocking collectives: 25.8 us -> 22.2 us
  Pallas kernels: 31.5 us -> 28.9 us
  starting transfers between devices: 8.06 us -> 9.98 us
  local copies, waits for them, and re-layouts: 1.84 us -> 0.08 us
    all_to_all x1, blocking collectives: 25.8 us -> 22.2 us  [local(): lax.all_to_all(send.reshape(count, 1, LANES), AXES, 0, 0, tiled=True)]
    pallas_call x4, Pallas kernels: 31.5 us -> 28.9 us  [the longest x1 14.7 us: local(): pl.pallas_call(second_kernel, in_specs=[HBM] + [VMEM] * 10, out_specs=[HB...]
    ppermute x2, starting transfers between devices: 8.06 us -> 9.98 us  [the longest x1 9.89 us: local(): from_odd = lax.ppermute(for_odd, AXES, odd_pairs)]
    slice x1 -> x0, local copies, waits for them, and re-layouts: 1.07 us -> none  [local(): below = lax.ppermute(pattern[:2 * H], AXES, backward_ring)]
    unnamed x4 -> x24, local copies, waits for them, and re-layouts: 0.77 us -> 0.08 us
  transfers between devices with their start and end apart: 2 -> 2, of which waited for: 0 -> 0; matrix products, arithmetic and copies ran while one was open for 1% -> 0% of each run, Pallas kernels for 16% -> 18%
where the time goes in v1:
time: 62.4 us; the launch traced here: 62.2 us
  Pallas kernels  28.9 us (46%)
  blocking collectives  22.2 us (36%)
  starting transfers between devices  9.98 us (16%)
  between operations  1.02 us (2%)
    all_to_all x1, blocking collectives, local(): lax.all_to_all(send.reshape(count, 1, LANES), AXES, 0, 0, tiled=True)  22.2 us
    pallas_call x1, Pallas kernels, local(): pl.pallas_call(second_kernel, in_specs=[HBM] + [VMEM] * 10, out_specs=[HB...  14.7 us
    pallas_call x1, Pallas kernels, local(): pl.pallas_call(first_kernel, in_specs=[HBM] * 5, out_specs=[HBM, VMEM], o...  11.3 us
    ppermute x1, starting transfers between devices, local(): from_odd = lax.ppermute(for_odd, AXES, odd_pairs)  9.89 us
    pallas_call x1, Pallas kernels, local(): pl.pallas_call(rims_kernel, in_specs=[HBM], out_specs=[VMEM] * 2, out_sha...  1.91 us
  transfers between devices with their start and end apart: 2, of which 0 were waited for; matrix products, arithmetic and copies ran while one was open for 0% of the time, Pallas kernels for 18%

profile of v1, /device:TPU:1, one launch (start us, length us, event | category | flops | bytes accessed | tf_op | source)
XLA Modules:
  0.0 62.2 jit_solution(15340201768960533639)
XLA Ops:
  0.6 0.0 copy-start
  0.6 0.0 copy-start.1
  0.7 0.0 copy-start.4
  0.7 0.0 copy-start.8
  0.7 1.9 %rims.1 = (s32[32,2048]{1,0:T(8,128)}, s32[32,2048]{1,0:T(8,128)}) custom-call(s32[512,2048]{1,0:T(8,128)} %pattern_hbm.3), custom_call_target="tpu_custom_call" | custom-call | tf_op jit(solution)/shard_map/rims/pallas_call | solution.py:341
  2.6 9.9 %collective-permute-start = (s32[32,2048]{1,0:T(8,128)}, s32[32,2048]{1,0:T(8,128)S(1)}, u32[]{:S(2)}, u32[]{:S(2)}) collective-permute-start(s32[32,2048]{1,0:T(8,128)} %get-tuple-element.9.for_odd_ref), channel_id=1, source_target_pairs={{0,0},{1,2},{2,1},{3,4},{4,3},{5,6},{6,5},{7,8},{8,7},{9,10},{10,9... | collective-permute-start | bytes 786440 | tf_op jit(solution)/shard_map/ppermute | solution.py:349
  12.5 0.0 copy-start.2
  12.5 0.0 copy-start.3
  12.5 0.0 copy-start.5
  12.5 0.0 copy-start.6
  12.5 0.0 copy-start.7
  12.6 0.0 copy-start.9
  12.6 0.0 copy-start.10
  12.6 0.0 copy-start.11
  12.6 0.1 collective-permute-start.1
  12.7 0.0 copy-done
  12.7 0.0 copy-done.1
  12.7 0.0 copy-done.4
  12.7 0.0 copy-done.8
  12.7 11.3 %first_blur.1 = (f32[512,2048]{1,0:T(8,128)}, f32[8,2048]{1,0:T(8,128)S(1)}) custom-call(s32[512,2048]{1,0:T(8,128)} %pattern_hbm.3, bf16[448,256]{1,0:T(8,128)(2,1)S(1)} %copy-done.8, bf16[64,64]{1,0:T(8,128)(2,1)S(1)} %copy-done.4, bf16[512,256]{1,0:T(8,128)(2,1)S(1)} %copy-done.1, bf16[512,256]{1,0:T(8,128)(2,1)S(1)} %copy-done), custom_call_target="tpu_custom_call" | custom-call | flops 6000000000 | bytes 30000000 | tf_op jit(solution)/shard_map/first_blur/pallas_call | solution.py:356
  24.0 0.0 collective-permute-done.from_odd_ref
  24.0 0.0 collective-permute-done.1.from_even_ref
  24.1 0.0 copy-done.2
  24.1 0.0 copy-done.3
  24.1 1.1 %edge_blur.1 = (f32[64,2048]{1,0:T(8,128)S(1)}, f32[256,128]{1,0:T(8,128)S(1)}) custom-call(s32[32,2048]{1,0:T(8,128)S(1)} %copy-done.2, s32[32,2048]{1,0:T(8,128)S(1)} %copy-done.3, s32[32,2048]{1,0:T(8,128)S(1)} %collective-permute-done.from_odd_ref, s32[32,2048]{1,0:T(8,128)S(1)} %collective-permute-done.1.from_even_ref, ...), custom_call_target="tpu_custom_call" | custom-call | tf_op jit(solution)/shard_map/edge_blur/pallas_call | solution.py:372
  25.1 22.2 %all_to_all.5 = f32[256,1,128]{2,1,0:T(1,128)S(1)} all-to-all(f32[256,1,128]{2,1,0:T(1,128)S(1)} %bitcast.5), channel_id=1, replica_groups=mesh['band'=16,'strip'=16] {'band','strip'}, dimensions={0} | all-to-all | bytes 262144 | tf_op jit(solution)/shard_map/all_to_all | solution.py:381
  47.3 0.0 copy-done.5
  47.3 0.0 copy-done.6
  47.4 0.0 copy-done.7
  47.4 0.0 copy-done.9
  47.4 0.0 copy-done.10
  47.4 0.0 copy-done.11
  47.4 14.7 %second_blur.1 = (f32[512,2048]{1,0:T(8,128)}, f32[512,2048]{1,0:T(8,128)}) custom-call(f32[512,2048]{1,0:T(8,128)} %get-tuple-element.8.now_hbm, f32[64,2048]{1,0:T(8,128)S(1)} %get-tuple-element.12.edge_ref, f32[256,128]{1,0:T(8,128)S(1)} %bitcast.4, bf16[128,384]{1,0:T(8,128)(2,1)S(1)} %copy-done.10, bf16[128,384]{1,0:T(8,128)(2,1)S(1)} %copy-done.9, ...), custom_call_target="tpu_custom_call" | custom-call | flops 8000000000 | bytes 30000000 | tf_op jit(solution)/shard_map/second_blur/pallas_call | solution.py:399
Async XLA Ops:
  0.6 12.1 %copy-start = (bf16[512,256]{1,0:T(8,128)(2,1)S(1)}, bf16[512,256]{1,0:T(8,128)(2,1)}, u32[]{:S(2)}) copy-start(bf16[512,256]{1,0:T(8,128)(2,1)} %constant.21.clone.wl_hbm.wl_ref) | copy-start | bytes 786436
  0.6 12.1 %copy-start.1 = (bf16[512,256]{1,0:T(8,128)(2,1)S(1)}, bf16[512,256]{1,0:T(8,128)(2,1)}, u32[]{:S(2)}) copy-start(bf16[512,256]{1,0:T(8,128)(2,1)} %constant.20.clone.wh_hbm.wh_ref) | copy-start | bytes 786436
  0.7 12.1 %copy-start.4 = (bf16[64,64]{1,0:T(8,128)(2,1)S(1)}, bf16[64,64]{1,0:T(8,128)(2,1)}, u32[]{:S(2)}) copy-start(bf16[64,64]{1,0:T(8,128)(2,1)} %constant.23.clone.small_hbm.taps_ref) | copy-start | bytes 24580
  0.7 12.1 %copy-start.8 = (bf16[448,256]{1,0:T(8,128)(2,1)S(1)}, bf16[448,256]{1,0:T(8,128)(2,1)}, u32[]{:S(2)}) copy-start(bf16[448,256]{1,0:T(8,128)(2,1)} %constant.22.clone.big_hbm) | copy-start | bytes 688132
  2.6 21.4 %collective-permute-start = (s32[32,2048]{1,0:T(8,128)}, s32[32,2048]{1,0:T(8,128)S(1)}, u32[]{:S(2)}, u32[]{:S(2)}) collective-permute-start(s32[32,2048]{1,0:T(8,128)} %get-tuple-element.9.for_odd_ref), channel_id=1, source_target_pairs={{0,0},{1,2},{2,1},{3,4},{4,3},{5,6},{6,5},{7,8},{8,7},{9,10},{10,9... | collective-permute-start | bytes 786440 | tf_op jit(solution)/shard_map/ppermute | solution.py:349
  12.5 11.6 %copy-start.2 = (s32[32,2048]{1,0:T(8,128)S(1)}, s32[32,2048]{1,0:T(8,128)}, u32[]{:S(2)}) copy-start(s32[32,2048]{1,0:T(8,128)} %get-tuple-element.9.for_odd_ref) | copy-start | bytes 786436
  12.5 11.6 %copy-start.3 = (s32[32,2048]{1,0:T(8,128)S(1)}, s32[32,2048]{1,0:T(8,128)}, u32[]{:S(2)}) copy-start(s32[32,2048]{1,0:T(8,128)} %get-tuple-element.10.for_even_ref) | copy-start | bytes 786436
  12.5 34.8 %copy-start.5 = (bf16[256,768]{1,0:T(8,128)(2,1)S(1)}, bf16[256,768]{1,0:T(8,128)(2,1)}, u32[]{:S(2)}) copy-start(bf16[256,768]{1,0:T(8,128)(2,1)} %constant.27.clone.kerl_ref) | copy-start | bytes 1179652
  12.5 34.8 %copy-start.6 = (bf16[256,768]{1,0:T(8,128)(2,1)S(1)}, bf16[256,768]{1,0:T(8,128)(2,1)}, u32[]{:S(2)}) copy-start(bf16[256,768]{1,0:T(8,128)(2,1)} %constant.26.clone.kerh_ref) | copy-start | bytes 1179652
  12.5 34.8 %copy-start.7 = (bf16[448,256]{1,0:T(8,128)(2,1)S(1)}, bf16[448,256]{1,0:T(8,128)(2,1)}, u32[]{:S(2)}) copy-start(bf16[448,256]{1,0:T(8,128)(2,1)} %constant.28.clone.big_ref) | copy-start | bytes 688132
  12.6 34.8 %copy-start.9 = (bf16[128,384]{1,0:T(8,128)(2,1)S(1)}, bf16[128,384]{1,0:T(8,128)(2,1)}, u32[]{:S(2)}) copy-start(bf16[128,384]{1,0:T(8,128)(2,1)} %constant.25.clone.mixl_ref) | copy-start | bytes 294916
  12.6 34.8 %copy-start.10 = (bf16[128,384]{1,0:T(8,128)(2,1)S(1)}, bf16[128,384]{1,0:T(8,128)(2,1)}, u32[]{:S(2)}) copy-start(bf16[128,384]{1,0:T(8,128)(2,1)} %constant.24.clone.mixh_ref) | copy-start | bytes 294916
  12.6 34.8 %copy-start.11 = (bf16[128,96]{1,0:T(8,128)(2,1)S(1)}, bf16[128,96]{1,0:T(8,128)(2,1)}, u32[]{:S(2)}) copy-start(bf16[128,96]{1,0:T(8,128)(2,1)} %constant.29.clone.small_ref) | copy-start | bytes 73732
  12.6 11.5 %collective-permute-start.1 = (s32[32,2048]{1,0:T(8,128)}, s32[32,2048]{1,0:T(8,128)S(1)}, u32[]{:S(2)}, u32[]{:S(2)}) collective-permute-start(s32[32,2048]{1,0:T(8,128)} %get-tuple-element.10.for_even_ref), channel_id=1, source_target_pairs={{0,1},{1,0},{2,3},{3,2},{4,5},{5,4},{6,7},{7,6},{8,9},{9,8},{10,11... | collective-permute-start | bytes 786440 | tf_op jit(solution)/shard_map/ppermute | solution.py:350

commit v2 on v1

--- a/solution.py
+++ b/solution.py
@@ -99,82 +99,69 @@
     return jnp.sum(value, axis=0, keepdims=True)
 
 
-def rims_kernel(pattern_hbm, odd_ref, even_ref, sem):
-    rows, rim = pattern_hbm.shape[0], odd_ref.shape[0]
-    last = rows - rim
-    odd = lax.rem(lax.axis_index(AXES), 2)
-    copies = [
-        pltpu.make_async_copy(pattern_hbm.at[pl.ds(pl.multiple_of(start, rim), rim)], ref, sem.at[i])
-        for i, (ref, start) in enumerate(((odd_ref, odd * last), (even_ref, (1 - odd) * last)))
-    ]
-    for copy in copies:
-        copy.start()
-    for copy in copies:
-        copy.wait()
-
-
-def first_kernel(
-    pattern_hbm, big_hbm, small_hbm, wh_hbm, wl_hbm, out_hbm, sums_ref,
-    pattern_ref, out_ref, big_ref, small_ref, wh_ref, wl_ref, rh, rl, in_sem, out_sem, taps_sem,
-):
+def windows(first, last, wide):
+    return [(at, min(at + wide, last)) for at in range(first, last, wide)]
+
+
+def rims_kernel(pattern_ref, odd_ref, even_ref):
+    even = lax.rem(lax.axis_index(AXES), 2) == 0
+    top, bottom = pattern_ref[: 2 * H], pattern_ref[pattern_ref.shape[0] - 2 * H :]
+    odd_ref[...] = jnp.where(even, top, bottom)
+    even_ref[...] = jnp.where(even, bottom, top)
+
+
+def cut(packed_ref):
+    column = POOL + 2 * LANES
+    tall = 2 * (POOL - 2 * H)
+    at = 2 * column + tall
+    return packed_ref[:column], packed_ref[column : 2 * column], packed_ref[2 * column : at], packed_ref[at : at + 4 * H, : 4 * H]
+
+
+def first_kernel(pattern_ref, taps_ref, out_ref, sums_ref, rh, rl):
+    wh, wl, big, small = cut(taps_ref)
     rows, width = pattern_ref.shape
     cells = width // POOL
-    big = big_ref.shape[1]
-    wide = big - 2 * H
+    clear_rims(rh)
+    clear_rims(rl)
+    parts = windows(H, rows - H, big.shape[1] - 2 * H)
+    zeros = jnp.zeros((H, width), F32)
+    out_ref[:H] = zeros
+    out_ref[rows - H :] = zeros
 
     def cell(t):
         return slice(POOL * t, POOL * (t + 1))
-
-    loads = [pltpu.make_async_copy(pattern_hbm.at[:, cell(t)], pattern_ref.at[:, cell(t)], in_sem.at[t]) for t in range(cells)]
-    stores = [pltpu.make_async_copy(out_ref.at[:, cell(t)], out_hbm.at[:, cell(t)], out_sem.at[t]) for t in range(cells)]
-    pairs = ((big_hbm, big_ref), (small_hbm, small_ref), (wh_hbm, wh_ref), (wl_hbm, wl_ref))
-    taps_loads = [pltpu.make_async_copy(hbm, ref, taps_sem.at[i]) for i, (hbm, ref) in enumerate(pairs)]
-    for load in loads[:1] + taps_loads + loads[1:]:
-        load.start()
-    clear_rims(rh)
-    clear_rims(rl)
-    for load in taps_loads:
-        load.wait()
 
     def down(t):
         here = slice(POOL * t + LANES, POOL * (t + 1) + LANES)
         _, level = pixels(pattern_ref[:, cell(t)])
         x = level.astype(BF16)
-        at = 0
-        while at + 2 * H < rows:
-            taps = big_ref[...] if at + big <= rows else small_ref[...]
-            part = blur_down(taps, x[at : at + taps.shape[1]])
-            rh[at : at + part.shape[0], here], rl[at : at + part.shape[0], here] = split(part)
-            at += wide
+        for first, last in parts:
+            taps = big if last - first + 2 * H == big.shape[1] else small
+            part = blur_down(taps, x[first - H : last + H])
+            rh[first - H : last - H, here], rl[first - H : last - H, here] = split(part)
 
     def across(t):
         window = slice(POOL * t, POOL * (t + 1) + 2 * LANES)
-        forward = blur_across(rh[:, window], rl[:, window], wh_ref[...], wl_ref[...])
+        forward = blur_across(rh[:, window], rl[:, window], wh, wl)
         kind, level = pixels(pattern_ref[:, cell(t)])
         now = jnp.maximum(1.5 * kind[H : rows - H] - forward, 0.0)
-        zeros = jnp.zeros((H, POOL), F32)
-        out_ref[:H, cell(t)] = zeros
         out_ref[H : rows - H, cell(t)] = now
-        out_ref[rows - H :, cell(t)] = zeros
         sums = [column_sums(now[: POOL - H]), column_sums(now[POOL - H :])]
         sums += [column_sums(value[first : first + POOL]) for value in (level, kind) for first in (0, POOL)]
         sums_ref[:, cell(t)] = jnp.concatenate(sums + [jnp.zeros((2, POOL), F32)], axis=0)
-        stores[t].start()
 
     for t in range(cells + 1):
         if t < cells:
-            loads[t].wait()
             down(t)
         if t > 0:
             across(t - 1)
-    for store in stores:
-        store.wait()
-
-
-def edge_kernel(for_odd_ref, for_even_ref, from_odd_ref, from_even_ref, sums_ref, taps_ref, wh_ref, wl_ref, edge_ref, send_ref):
+
+
+def edge_kernel(for_odd_ref, for_even_ref, from_odd_ref, from_even_ref, sums_ref, taps_ref, edge_ref, send_ref):
     count = lax.axis_size(AXES)
     me = lax.axis_index(AXES)
     width = edge_ref.shape[1]
+    wh, wl, _, taps = cut(taps_ref)
     cells = width // POOL
     even = lax.rem(me, 2) == 0
     top = jnp.where(even, for_odd_ref[...], for_even_ref[...])
@@ -185,13 +172,13 @@
     below = jnp.where(me < count - 1, below, 0)
     upper = jnp.concatenate([above, top], axis=0)
     lower = jnp.concatenate([bottom, below], axis=0)
-    blurred = [blur_down(taps_ref[...], pixels(p)[1].astype(BF16)) for p in (upper, lower)]
+    blurred = [blur_down(taps, pixels(p)[1].astype(BF16)) for p in (upper, lower)]
     rim = jnp.zeros((4 * H, LANES), BF16)
     wide = [jnp.concatenate([rim, part, rim], axis=1) for part in split(jnp.concatenate(blurred, axis=0))]
     stacked = [
         jnp.concatenate([w[:, POOL * j : POOL * (j + 1) + 2 * LANES] for j in range(cells)], axis=0) for w in wide
     ]
-    forward = blur_across(stacked[0], stacked[1], wh_ref[...], wl_ref[...])
+    forward = blur_across(stacked[0], stacked[1], wh, wl)
     kind = jnp.concatenate([upper[H : 3 * H], lower[H : 3 * H]], axis=0).astype(F32)
     row = lax.broadcasted_iota(jnp.int32, (8, POOL), 0)
     place = lax.broadcasted_iota(jnp.int32, (8, LANES), 0)
@@ -243,9 +230,9 @@
 
 
 def second_kernel(
-    now_hbm, edge_ref, all_ref, mixh_ref, mixl_ref, kerh_ref, kerl_ref, big_ref, small_ref, wh_ref, wl_ref,
+    now_ref, edge_ref, all_ref, mixh_ref, mixl_ref, kerh_ref, kerl_ref, big_ref, small_ref, wh_ref, wl_ref,
     dose_hbm, exposure_hbm,
-    now_ref, dose_ref, exposure_ref, rh, rl, up_ref, b1_ref, b2_ref, in_sem, dose_sem, exposure_sem,
+    dose_ref, exposure_ref, rh, rl, up_ref, b1_ref, b2_ref, dose_sem, exposure_sem,
 ):
     rows, width = now_ref.shape
     cells = width // POOL
@@ -255,67 +242,64 @@
     def cell(t):
         return slice(POOL * t, POOL * (t + 1))
 
-    loads = [pltpu.make_async_copy(now_hbm.at[:, cell(t)], now_ref.at[:, cell(t)], in_sem.at[t]) for t in range(cells)]
+    parts = windows(0, rows, wide)
     stores = [
-        [pltpu.make_async_copy(ref.at[:, cell(t)], hbm.at[:, cell(t)], sem.at[t]) for t in range(cells)]
+        [pltpu.make_async_copy(ref.at[a:b], hbm.at[a:b], sem.at[i]) for i, (a, b) in enumerate(parts)]
         for ref, hbm, sem in ((dose_ref, dose_hbm, dose_sem), (exposure_ref, exposure_hbm, exposure_sem))
     ]
-    for load in loads:
-        load.start()
     clear_rims(rh)
     clear_rims(rl)
     find_back(
         lax.axis_index(AXES), all_ref, (mixh_ref[...], mixl_ref[...]), (kerh_ref[...], kerl_ref[...]), up_ref, b1_ref, b2_ref
     )
 
-    def down(t):
-        here = slice(POOL * t + LANES, POOL * (t + 1) + LANES)
-        edge = edge_ref[:, cell(t)]
-        pieces = [
-            (edge[:H], 0),
-            (edge[H : 2 * H], 1),
-            (now_ref[H:POOL, cell(t)], 1),
-            (now_ref[POOL : rows - H, cell(t)], 2),
-            (edge[2 * H : 3 * H], 2),
-            (edge[3 * H :], 3),
-        ]
-        doses, at = [], -H
-        for value, line in pieces:
+    runs = [
+        (-H, 0, edge_ref, 0, 0),
+        (0, H, edge_ref, H, 1),
+        (H, POOL, now_ref, H, 1),
+        (POOL, rows - H, now_ref, POOL, 2),
+        (rows - H, rows, edge_ref, 2 * H, 2),
+        (rows, rows + H, edge_ref, 3 * H, 3),
+    ]
+
+    def dose_rows(first, last, t):
+        doses = []
+        for start, stop, ref, at, line in runs:
+            a, b = max(start, first), min(stop, last)
+            if a >= b:
+                continue
+            value = ref[at + a - start : at + b - start, cell(t)]
             second = value > MIDDLE
             dose = value - up_ref[line : line + 1, cell(t)]
             dose = jnp.maximum(jnp.where(second, dose - LIFT, dose), 0.0)
             doses.append(dose)
-            if 0 <= at < rows:
+            low, high = max(a, first + H), min(b, last - H)
+            if low < high:
                 base = jnp.where(dose > 0, dose + jnp.where(second, 0.55, 0.5), 0.0)
-                dose_ref[at : at + value.shape[0], cell(t)] = base
-            at += value.shape[0]
-        high, low = split(jnp.concatenate(doses, axis=0))
-        at = 0
-        while at < rows:
-            taps = big_ref[...] if at + big <= rows + 2 * H else small_ref[...]
-            depth = taps.shape[1]
-            part = blur_down3(taps, high[at : at + depth], low[at : at + depth])
-            rh[at : at + part.shape[0], here], rl[at : at + part.shape[0], here] = split(part)
-            at += wide
-
-    def across(t):
-        window = slice(POOL * t, POOL * (t + 1) + 2 * LANES)
-        forward = blur_across(rh[:, window], rl[:, window], wh_ref[...], wl_ref[...])
-        for half in range(rows // POOL):
-            these = slice(POOL * half, POOL * (half + 1))
-            exposure = forward[these] + up_ref[4 + half : 5 + half, cell(t)]
-            base = dose_ref[these, cell(t)]
-            exposure_ref[these, cell(t)] = exposure
-            dose_ref[these, cell(t)] = jnp.where(base > 0, base - exposure, 0.0)
+                dose_ref[low:high, cell(t)] = base[low - a : high - a]
+        return jnp.concatenate(doses, axis=0)
+
+    for i, (first, last) in enumerate(parts):
+        taps = big_ref[...] if last - first == wide else small_ref[...]
+        for t in range(cells + 1):
+            if t < cells:
+                here = slice(POOL * t + LANES, POOL * (t + 1) + LANES)
+                part = blur_down3(taps, *split(dose_rows(first - H, last + H, t)))
+                rh[first:last, here], rl[first:last, here] = split(part)
+            if t > 0:
+                here = cell(t - 1)
+                window = slice(POOL * (t - 1), POOL * t + 2 * LANES)
+                forward = blur_across(rh[first:last, window], rl[first:last, window], wh_ref[...], wl_ref[...])
+                for half in range(rows // POOL):
+                    a, b = max(first, POOL * half), min(last, POOL * (half + 1))
+                    if a >= b:
+                        continue
+                    exposure = forward[a - first : b - first] + up_ref[4 + half : 5 + half, here]
+                    base = dose_ref[a:b, here]
+                    exposure_ref[a:b, here] = exposure
+                    dose_ref[a:b, here] = jnp.where(base > 0, base - exposure, 0.0)
         for group in stores:
-            group[t].start()
-
-    for t in range(cells + 1):
-        if t < cells:
-            loads[t].wait()
-            down(t)
-        if t > 0:
-            across(t - 1)
+            group[i].start()
     for group in stores:
         for store in group:
             store.wait()
@@ -340,10 +324,10 @@
     even_pairs = [(i, i ^ 1) for i in range(count)]
     for_odd, for_even = pl.pallas_call(
         rims_kernel,
-        in_specs=[HBM],
+        in_specs=[VMEM],
         out_specs=[VMEM] * 2,
         out_shape=[jax.ShapeDtypeStruct((2 * H, width), pattern.dtype)] * 2,
-        scratch_shapes=[pltpu.SemaphoreType.DMA((2,))],
+        compiler_params=params(40),
         name="rims",
     )(pattern)
     from_odd = lax.ppermute(for_odd, AXES, odd_pairs)
@@ -351,32 +335,29 @@
 
     taps_high, taps_low = (jnp.asarray(m) for m in column_taps(1.0 / TOTAL))
 
-    big = jnp.asarray(row_taps(wide, 0.2))
-    small = jnp.asarray(row_taps((rows - 2 * H) % wide, 0.2))
+    assert (rows - 2 * H) % wide in (0, 2 * H)
+    short = row_taps(2 * H, 0.2)
+    short = np.concatenate([short, np.zeros((short.shape[0], POOL - short.shape[1]), short.dtype)], axis=1)
+    first_taps = jnp.asarray(np.concatenate([*column_taps(1.0 / TOTAL), row_taps(wide, 0.2), short], axis=0))
     now, sums = pl.pallas_call(
         first_kernel,
-        in_specs=[HBM] * 5,
-        out_specs=[HBM, VMEM],
+        in_specs=[VMEM] * 2,
+        out_specs=[VMEM] * 2,
         out_shape=[jax.ShapeDtypeStruct((rows, width), F32), jax.ShapeDtypeStruct((8, width), F32)],
-        scratch_shapes=[pltpu.VMEM((rows, width), jnp.int32), pltpu.VMEM((rows, width), F32)]
-        + [pltpu.VMEM(m.shape, BF16) for m in (big, small, taps_high, taps_low)]
-        + [pltpu.VMEM((rows - 2 * H, padded), BF16)] * 2
-        + [pltpu.SemaphoreType.DMA((cells,))] * 2
-        + [pltpu.SemaphoreType.DMA((4,))],
-        compiler_params=params(52),
+        scratch_shapes=[pltpu.VMEM((rows - 2 * H, padded), BF16)] * 2,
+        compiler_params=params(40),
         cost_estimate=pl.CostEstimate(flops=6 * 10**9, bytes_accessed=3 * 10**7, transcendentals=0),
         name="first_blur",
-    )(pattern, big, small, taps_high, taps_low)
-
-    edge_taps = jnp.asarray(row_taps(2 * H, 0.2))
+    )(pattern, first_taps)
+
     edge, send = pl.pallas_call(
         edge_kernel,
-        in_specs=[VMEM] * 8,
+        in_specs=[VMEM] * 6,
         out_specs=[VMEM] * 2,
         out_shape=[jax.ShapeDtypeStruct((4 * H, width), F32), jax.ShapeDtypeStruct((count, LANES), F32)],
         compiler_params=params(40),
         name="edge_blur",
-    )(for_odd, for_even, from_odd, from_even, sums, edge_taps, taps_high, taps_low)
+    )(for_odd, for_even, from_odd, from_even, sums, first_taps)
 
     gathered = lax.all_to_all(send.reshape(count, 1, LANES), AXES, 0, 0, tiled=True).reshape(count, LANES)
 
@@ -398,15 +379,15 @@
     small = jnp.asarray(row_taps(rows % wide, 1.0))
     return pl.pallas_call(
         second_kernel,
-        in_specs=[HBM] + [VMEM] * 10,
+        in_specs=[VMEM] * 11,
         out_specs=[HBM] * 2,
         out_shape=[jax.ShapeDtypeStruct((rows, width), F32)] * 2,
-        scratch_shapes=[pltpu.VMEM((rows, width), F32)] * 3
+        scratch_shapes=[pltpu.VMEM((rows, width), F32)] * 2
         + [pltpu.VMEM((rows, padded), BF16)] * 2
         + [pltpu.VMEM((8, width), F32)]
         + [pltpu.VMEM((count, LANES), F32)] * 2
-        + [pltpu.SemaphoreType.DMA((cells,))] * 3,
-        compiler_params=params(50),
+        + [pltpu.SemaphoreType.DMA((cells,))] * 2,
+        compiler_params=params(44),
         cost_estimate=pl.CostEstimate(flops=8 * 10**9, bytes_accessed=3 * 10**7, transcendentals=0),
         name="second_blur",
     )(now, edge, gathered, *constants, big, small, taps_high, taps_low)

time: 62.4 us -> 53.3 us (0.85)
  Pallas kernels: 28.9 us -> 15.3 us
  local copies, waits for them, and re-layouts: 0.08 us -> 2.24 us
  blocking collectives: 22.2 us -> 23.5 us
  waiting for transfers between devices: 0.01 us -> 1.02 us
    pallas_call x4, Pallas kernels: 28.9 us -> 15.3 us  [the longest x1 9.42 us: local(): pl.pallas_call(second_kernel, in_specs=[VMEM] * 11, out_specs=[HBM] * 2,...]
    unnamed x24 -> x20, local copies, waits for them, and re-layouts: 0.08 us -> 2.24 us
    all_to_all x1, blocking collectives: 22.2 us -> 23.5 us  [local(): lax.all_to_all(send.reshape(count, 1, LANES), AXES, 0, 0, tiled=True)]
    ppermute x1, waiting for transfers between devices: 0.01 us -> 1.02 us  [local(): from_odd = lax.ppermute(for_odd, AXES, odd_pairs)]
  transfers between devices with their start and end apart: 2 -> 2, of which waited for: 0 -> 1; matrix products, arithmetic and copies ran while one was open for 0% -> 0% of each run, Pallas kernels for 18% -> 9%
where the time goes in v2:
time: 53.3 us; the launch traced here: 53.2 us
  blocking collectives  23.5 us (44%)
  Pallas kernels  15.3 us (29%)
  starting transfers between devices  10.1 us (19%)
  local copies, waits for them, and re-layouts  2.24 us (4%)
  waiting for transfers between devices  1.02 us (2%)
  between operations  0.95 us (2%)
    all_to_all x1, blocking collectives, local(): lax.all_to_all(send.reshape(count, 1, LANES), AXES, 0, 0, tiled=True)  23.5 us
    ppermute x1, starting transfers between devices, local(): from_odd = lax.ppermute(for_odd, AXES, odd_pairs)  10 us
    pallas_call x1, Pallas kernels, local(): pl.pallas_call(second_kernel, in_specs=[VMEM] * 11, out_specs=[HBM] * 2,...  9.42 us
    pallas_call x1, Pallas kernels, local(): pl.pallas_call(first_kernel, in_specs=[VMEM] * 2, out_specs=[VMEM] * 2, o...  4.76 us
    unnamed x20, local copies, waits for them, and re-layouts  2.24 us
    pallas_call x1, Pallas kernels, local(): pl.pallas_call(edge_kernel, in_specs=[VMEM] * 6, out_specs=[VMEM] * 2, ou...  1.07 us
  transfers between devices with their start and end apart: 2, of which 1 were waited for; matrix products, arithmetic and copies ran while one was open for 0% of the time, Pallas kernels for 9%

profile of v2, /device:TPU:1, one launch (start us, length us, event | category | flops | bytes accessed | tf_op | source)
XLA Modules:
  0.0 53.2 jit_solution(8025903938251738867)
XLA Ops:
  0.6 0.0 copy-start
  0.6 2.2 %copy-done = s32[512,2048]{1,0:T(8,128)S(1)} copy-done((s32[512,2048]{1,0:T(8,128)S(1)}, s32[512,2048]{1,0:T(8,128)}, u32[]{:S(2)}) %copy-start) | copy-done | bytes 4194328
  2.8 0.0 copy-start.1
  2.8 0.1 rims.1
  2.9 10.0 %collective-permute-start = (s32[32,2048]{1,0:T(8,128)S(1)}, s32[32,2048]{1,0:T(8,128)S(1)}, u32[]{:S(2)}, u32[]{:S(2)}) collective-permute-start(s32[32,2048]{1,0:T(8,128)S(1)} %get-tuple-element.9.for_odd_ref), channel_id=1, source_target_pairs={{0,0},{1,2},{2,1},{3,4},{4,3},{5,6},{6,5},{7,8},{8,7},{9,10},{10,9... | collective-permute-start | bytes 786440 | tf_op jit(solution)/shard_map/ppermute | solution.py:333
  12.9 0.0 copy-start.2
  12.9 0.0 copy-start.3
  12.9 0.0 copy-start.4
  12.9 0.0 copy-start.5
  13.0 0.0 copy-start.6
  13.0 0.0 copy-start.7
  13.0 0.0 copy-start.8
  13.0 0.0 copy-start.9
  13.0 0.1 collective-permute-start.1
  13.1 0.0 copy-done.1
  13.1 4.8 %first_blur.1 = (f32[512,2048]{1,0:T(8,128)S(1)}, f32[8,2048]{1,0:T(8,128)S(1)}) custom-call(s32[512,2048]{1,0:T(8,128)S(1)} %copy-done, bf16[1536,256]{1,0:T(8,128)(2,1)S(1)} %copy-done.1), custom_call_target="tpu_custom_call" | custom-call | flops 6000000000 | bytes 30000000 | tf_op jit(solution)/shard_map/first_blur/pallas_call | solution.py:342
  17.9 1.0 %collective-permute-done.from_odd_ref = s32[32,2048]{1,0:T(8,128)S(1)} collective-permute-done((s32[32,2048]{1,0:T(8,128)S(1)}, s32[32,2048]{1,0:T(8,128)S(1)}, u32[]{:S(2)}, u32[]{:S(2)}) %collective-permute-start) | collective-permute-done | bytes 262176 | tf_op jit(solution)/shard_map/ppermute | solution.py:333
  18.9 0.0 collective-permute-done.1.from_even_ref
  18.9 1.1 %edge_blur.1 = (f32[64,2048]{1,0:T(8,128)S(1)}, f32[256,128]{1,0:T(8,128)S(1)}) custom-call(s32[32,2048]{1,0:T(8,128)S(1)} %get-tuple-element.9.for_odd_ref, s32[32,2048]{1,0:T(8,128)S(1)} %get-tuple-element.10.for_even_ref, s32[32,2048]{1,0:T(8,128)S(1)} %collective-permute-done.from_odd_ref, s32[32,2048]{1,0:T(8,128)S(1)} %collective-permute-done.1.from_even_ref, ...), custom_call_target="tpu_custom_call" | custom-call | tf_op jit(solution)/shard_map/edge_blur/pallas_call | solution.py:353
  20.0 23.5 %all_to_all.5 = f32[256,1,128]{2,1,0:T(1,128)S(1)} all-to-all(f32[256,1,128]{2,1,0:T(1,128)S(1)} %bitcast.5), channel_id=1, replica_groups=mesh['band'=16,'strip'=16] {'band','strip'}, dimensions={0} | all-to-all | bytes 262144 | tf_op jit(solution)/shard_map/all_to_all | solution.py:362
  43.5 0.0 copy-done.2
  43.5 0.0 copy-done.3
  43.5 0.0 copy-done.4
  43.5 0.0 copy-done.5
  43.5 0.0 copy-done.6
  43.6 0.0 copy-done.7
  43.6 0.0 copy-done.8
  43.6 0.0 copy-done.9
  43.6 9.4 %second_blur.1 = (f32[512,2048]{1,0:T(8,128)}, f32[512,2048]{1,0:T(8,128)}) custom-call(f32[512,2048]{1,0:T(8,128)S(1)} %get-tuple-element.8.now_ref, f32[64,2048]{1,0:T(8,128)S(1)} %get-tuple-element.12.edge_ref, f32[256,128]{1,0:T(8,128)S(1)} %bitcast.4, bf16[128,384]{1,0:T(8,128)(2,1)S(1)} %copy-done.8, bf16[128,384]{1,0:T(8,128)(2,1)S(1)} %copy-done.7, ...), custom_call_target="tpu_custom_call" | custom-call | flops 8000000000 | bytes 30000000 | tf_op jit(solution)/shard_map/second_blur/pallas_call | solution.py:380
Async XLA Ops:
  0.6 2.2 %copy-start = (s32[512,2048]{1,0:T(8,128)S(1)}, s32[512,2048]{1,0:T(8,128)}, u32[]{:S(2)}) copy-start(s32[512,2048]{1,0:T(8,128)} %pattern_ref.3) | copy-start | bytes 12582916
  2.8 10.3 %copy-start.1 = (bf16[1536,256]{1,0:T(8,128)(2,1)S(1)}, bf16[1536,256]{1,0:T(8,128)(2,1)}, u32[]{:S(2)}) copy-start(bf16[1536,256]{1,0:T(8,128)(2,1)} %constant.20.clone.taps_ref) | copy-start | bytes 2359300
  2.9 16.0 %collective-permute-start = (s32[32,2048]{1,0:T(8,128)S(1)}, s32[32,2048]{1,0:T(8,128)S(1)}, u32[]{:S(2)}, u32[]{:S(2)}) collective-permute-start(s32[32,2048]{1,0:T(8,128)S(1)} %get-tuple-element.9.for_odd_ref), channel_id=1, source_target_pairs={{0,0},{1,2},{2,1},{3,4},{4,3},{5,6},{6,5},{7,8},{8,7},{9,10},{10,9... | collective-permute-start | bytes 786440 | tf_op jit(solution)/shard_map/ppermute | solution.py:333
  12.9 30.6 %copy-start.2 = (bf16[256,768]{1,0:T(8,128)(2,1)S(1)}, bf16[256,768]{1,0:T(8,128)(2,1)}, u32[]{:S(2)}) copy-start(bf16[256,768]{1,0:T(8,128)(2,1)} %constant.24.clone.kerl_ref) | copy-start | bytes 1179652
  12.9 30.6 %copy-start.3 = (bf16[256,768]{1,0:T(8,128)(2,1)S(1)}, bf16[256,768]{1,0:T(8,128)(2,1)}, u32[]{:S(2)}) copy-start(bf16[256,768]{1,0:T(8,128)(2,1)} %constant.23.clone.kerh_ref) | copy-start | bytes 1179652
  12.9 30.6 %copy-start.4 = (bf16[512,256]{1,0:T(8,128)(2,1)S(1)}, bf16[512,256]{1,0:T(8,128)(2,1)}, u32[]{:S(2)}) copy-start(bf16[512,256]{1,0:T(8,128)(2,1)} %constant.19.clone.wl_ref) | copy-start | bytes 786436
  12.9 30.6 %copy-start.5 = (bf16[512,256]{1,0:T(8,128)(2,1)S(1)}, bf16[512,256]{1,0:T(8,128)(2,1)}, u32[]{:S(2)}) copy-start(bf16[512,256]{1,0:T(8,128)(2,1)} %constant.18.clone.wh_ref) | copy-start | bytes 786436
  13.0 30.6 %copy-start.6 = (bf16[448,256]{1,0:T(8,128)(2,1)S(1)}, bf16[448,256]{1,0:T(8,128)(2,1)}, u32[]{:S(2)}) copy-start(bf16[448,256]{1,0:T(8,128)(2,1)} %constant.25.clone.big_ref) | copy-start | bytes 688132
  13.0 30.6 %copy-start.7 = (bf16[128,384]{1,0:T(8,128)(2,1)S(1)}, bf16[128,384]{1,0:T(8,128)(2,1)}, u32[]{:S(2)}) copy-start(bf16[128,384]{1,0:T(8,128)(2,1)} %constant.22.clone.mixl_ref) | copy-start | bytes 294916
  13.0 30.6 %copy-start.8 = (bf16[128,384]{1,0:T(8,128)(2,1)S(1)}, bf16[128,384]{1,0:T(8,128)(2,1)}, u32[]{:S(2)}) copy-start(bf16[128,384]{1,0:T(8,128)(2,1)} %constant.21.clone.mixh_ref) | copy-start | bytes 294916
  13.0 30.6 %copy-start.9 = (bf16[128,96]{1,0:T(8,128)(2,1)S(1)}, bf16[128,96]{1,0:T(8,128)(2,1)}, u32[]{:S(2)}) copy-start(bf16[128,96]{1,0:T(8,128)(2,1)} %constant.26.clone.small_ref) | copy-start | bytes 73732
  13.0 5.9 %collective-permute-start.1 = (s32[32,2048]{1,0:T(8,128)S(1)}, s32[32,2048]{1,0:T(8,128)S(1)}, u32[]{:S(2)}, u32[]{:S(2)}) collective-permute-start(s32[32,2048]{1,0:T(8,128)S(1)} %get-tuple-element.10.for_even_ref), channel_id=1, source_target_pairs={{0,1},{1,0},{2,3},{3,2},{4,5},{5,4},{6,7},{7,6},{8,9},{9,8},{10,11... | collective-permute-start | bytes 786440 | tf_op jit(solution)/shard_map/ppermute | solution.py:334

commit v3 on v2

--- a/solution.py
+++ b/solution.py
@@ -103,11 +103,10 @@
     return [(at, min(at + wide, last)) for at in range(first, last, wide)]
 
 
-def rims_kernel(pattern_ref, odd_ref, even_ref):
+def rims_kernel(top_ref, bottom_ref, odd_ref, even_ref):
     even = lax.rem(lax.axis_index(AXES), 2) == 0
-    top, bottom = pattern_ref[: 2 * H], pattern_ref[pattern_ref.shape[0] - 2 * H :]
-    odd_ref[...] = jnp.where(even, top, bottom)
-    even_ref[...] = jnp.where(even, bottom, top)
+    odd_ref[...] = jnp.where(even, top_ref[...], bottom_ref[...])
+    even_ref[...] = jnp.where(even, bottom_ref[...], top_ref[...])
 
 
 def cut(packed_ref):
@@ -279,25 +278,32 @@
                 dose_ref[low:high, cell(t)] = base[low - a : high - a]
         return jnp.concatenate(doses, axis=0)
 
+    def across(first, last, ts):
+        spans = [slice(POOL * t, POOL * (t + 1) + 2 * LANES) for t in ts]
+        high, low = (jnp.concatenate([ref[first:last, span] for span in spans], axis=0) for ref in (rh, rl))
+        forward = blur_across(high, low, wh_ref[...], wl_ref[...])
+        for k, t in enumerate(ts):
+            here = cell(t)
+            for half in range(rows // POOL):
+                a, b = max(first, POOL * half), min(last, POOL * (half + 1))
+                if a >= b:
+                    continue
+                at = k * (last - first) + a - first
+                exposure = forward[at : at + b - a] + up_ref[4 + half : 5 + half, here]
+                base = dose_ref[a:b, here]
+                exposure_ref[a:b, here] = exposure
+                dose_ref[a:b, here] = jnp.where(base > 0, base - exposure, 0.0)
+
     for i, (first, last) in enumerate(parts):
-        taps = big_ref[...] if last - first == wide else small_ref[...]
-        for t in range(cells + 1):
-            if t < cells:
-                here = slice(POOL * t + LANES, POOL * (t + 1) + LANES)
-                part = blur_down3(taps, *split(dose_rows(first - H, last + H, t)))
-                rh[first:last, here], rl[first:last, here] = split(part)
-            if t > 0:
-                here = cell(t - 1)
-                window = slice(POOL * (t - 1), POOL * t + 2 * LANES)
-                forward = blur_across(rh[first:last, window], rl[first:last, window], wh_ref[...], wl_ref[...])
-                for half in range(rows // POOL):
-                    a, b = max(first, POOL * half), min(last, POOL * (half + 1))
-                    if a >= b:
-                        continue
-                    exposure = forward[a - first : b - first] + up_ref[4 + half : 5 + half, here]
-                    base = dose_ref[a:b, here]
-                    exposure_ref[a:b, here] = exposure
-                    dose_ref[a:b, here] = jnp.where(base > 0, base - exposure, 0.0)
+        full = last - first == wide
+        taps = big_ref[...] if full else small_ref[...]
+        for t in range(cells):
+            here = slice(POOL * t + LANES, POOL * (t + 1) + LANES)
+            part = blur_down3(taps, *split(dose_rows(first - H, last + H, t)))
+            rh[first:last, here], rl[first:last, here] = split(part)
+            if full and t > 0:
+                across(first, last, [t - 1])
+        across(first, last, [cells - 1] if full else list(range(cells)))
         for group in stores:
             group[i].start()
     for group in stores:
@@ -322,14 +328,17 @@
 
     odd_pairs = [(i, i if i in (0, count - 1) else ((i + 1) ^ 1) - 1) for i in range(count)]
     even_pairs = [(i, i ^ 1) for i in range(count)]
+    strip = (2 * H, width)
+    last_strip = rows // (2 * H) - 1
     for_odd, for_even = pl.pallas_call(
         rims_kernel,
-        in_specs=[VMEM],
+        grid=(1,),
+        in_specs=[pl.BlockSpec(strip, lambda i: (0, 0)), pl.BlockSpec(strip, lambda i: (last_strip, 0))],
         out_specs=[VMEM] * 2,
-        out_shape=[jax.ShapeDtypeStruct((2 * H, width), pattern.dtype)] * 2,
-        compiler_params=params(40),
+        out_shape=[jax.ShapeDtypeStruct(strip, pattern.dtype)] * 2,
+        compiler_params=params(50),
         name="rims",
-    )(pattern)
+    )(pattern, pattern)
     from_odd = lax.ppermute(for_odd, AXES, odd_pairs)
     from_even = lax.ppermute(for_even, AXES, even_pairs)
 

time: 53.3 us -> 52.1 us (0.977)
  local copies, waits for them, and re-layouts: 2.24 us -> 0.07 us
  Pallas kernels: 15.3 us -> 16.3 us
    unnamed x20, local copies, waits for them, and re-layouts: 2.24 us -> 0.07 us
    pallas_call x1, Pallas kernels: 0.06 us -> 1.24 us  [local(): pl.pallas_call(rims_kernel, grid=(1,), in_specs=[pl.BlockSpec(strip, lamb...]
where the time goes in v3:
time: 52.1 us; the launch traced here: 52 us
  blocking collectives  23.5 us (45%)
  Pallas kernels  16.3 us (31%)
  starting transfers between devices  10.1 us (19%)
  waiting for transfers between devices  1.02 us (2%)
  between operations  0.97 us (2%)
    all_to_all x1, blocking collectives, local(): lax.all_to_all(send.reshape(count, 1, LANES), AXES, 0, 0, tiled=True)  23.5 us
    ppermute x1, starting transfers between devices, local(): from_odd = lax.ppermute(for_odd, AXES, odd_pairs)  10 us
    pallas_call x1, Pallas kernels, local(): pl.pallas_call(second_kernel, in_specs=[VMEM] * 11, out_specs=[HBM] * 2,...  9.27 us
    pallas_call x1, Pallas kernels, local(): pl.pallas_call(first_kernel, in_specs=[VMEM] * 2, out_specs=[VMEM] * 2, o...  4.75 us
    pallas_call x1, Pallas kernels, local(): pl.pallas_call(rims_kernel, grid=(1,), in_specs=[pl.BlockSpec(strip, lamb...  1.24 us
    pallas_call x1, Pallas kernels, local(): pl.pallas_call(edge_kernel, in_specs=[VMEM] * 6, out_specs=[VMEM] * 2, ou...  1.06 us
  transfers between devices with their start and end apart: 2, of which 1 were waited for; matrix products, arithmetic and copies ran while one was open for 0% of the time, Pallas kernels for 9%

profile of v3, /device:TPU:1, one launch (start us, length us, event | category | flops | bytes accessed | tf_op | source)
XLA Modules:
  0.0 52.0 jit_solution(9717200432435064174)
XLA Ops:
  0.6 0.0 copy-start.1
  0.6 0.0 copy-start
  0.7 1.2 %rims.1 = (s32[32,2048]{1,0:T(8,128)S(1)}, s32[32,2048]{1,0:T(8,128)S(1)}) custom-call(s32[512,2048]{1,0:T(8,128)} %bottom_ref.1, s32[512,2048]{1,0:T(8,128)} %bottom_ref.1), custom_call_target="tpu_custom_call" | custom-call | tf_op jit(solution)/shard_map/rims/pallas_call | solution.py:333
  1.9 10.0 %collective-permute-start = (s32[32,2048]{1,0:T(8,128)S(1)}, s32[32,2048]{1,0:T(8,128)S(1)}, u32[]{:S(2)}, u32[]{:S(2)}) collective-permute-start(s32[32,2048]{1,0:T(8,128)S(1)} %get-tuple-element.9.for_odd_ref), channel_id=1, source_target_pairs={{0,0},{1,2},{2,1},{3,4},{4,3},{5,6},{6,5},{7,8},{8,7},{9,10},{10,9... | collective-permute-start | bytes 786440 | tf_op jit(solution)/shard_map/ppermute | solution.py:342
  11.9 0.0 copy-start.2
  11.9 0.0 copy-start.3
  11.9 0.0 copy-start.4
  12.0 0.0 copy-start.5
  12.0 0.0 copy-start.6
  12.0 0.0 copy-start.7
  12.0 0.0 copy-start.8
  12.0 0.0 copy-start.9
  12.0 0.1 collective-permute-start.1
  12.1 0.0 copy-done.1
  12.1 0.0 copy-done
  12.1 4.7 %first_blur.1 = (f32[512,2048]{1,0:T(8,128)S(1)}, f32[8,2048]{1,0:T(8,128)S(1)}) custom-call(s32[512,2048]{1,0:T(8,128)S(1)} %copy-done, bf16[1536,256]{1,0:T(8,128)(2,1)S(1)} %copy-done.1), custom_call_target="tpu_custom_call" | custom-call | flops 6000000000 | bytes 30000000 | tf_op jit(solution)/shard_map/first_blur/pallas_call | solution.py:351
  16.9 1.0 %collective-permute-done.from_odd_ref = s32[32,2048]{1,0:T(8,128)S(1)} collective-permute-done((s32[32,2048]{1,0:T(8,128)S(1)}, s32[32,2048]{1,0:T(8,128)S(1)}, u32[]{:S(2)}, u32[]{:S(2)}) %collective-permute-start) | collective-permute-done | bytes 262176 | tf_op jit(solution)/shard_map/ppermute | solution.py:342
  17.9 0.0 collective-permute-done.1.from_even_ref
  17.9 1.1 %edge_blur.1 = (f32[64,2048]{1,0:T(8,128)S(1)}, f32[256,128]{1,0:T(8,128)S(1)}) custom-call(s32[32,2048]{1,0:T(8,128)S(1)} %get-tuple-element.9.for_odd_ref, s32[32,2048]{1,0:T(8,128)S(1)} %get-tuple-element.10.for_even_ref, s32[32,2048]{1,0:T(8,128)S(1)} %collective-permute-done.from_odd_ref, s32[32,2048]{1,0:T(8,128)S(1)} %collective-permute-done.1.from_even_ref, ...), custom_call_target="tpu_custom_call" | custom-call | tf_op jit(solution)/shard_map/edge_blur/pallas_call | solution.py:362
  19.0 23.5 %all_to_all.5 = f32[256,1,128]{2,1,0:T(1,128)S(1)} all-to-all(f32[256,1,128]{2,1,0:T(1,128)S(1)} %bitcast.5), channel_id=1, replica_groups=mesh['band'=16,'strip'=16] {'band','strip'}, dimensions={0} | all-to-all | bytes 262144 | tf_op jit(solution)/shard_map/all_to_all | solution.py:371
  42.5 0.0 copy-done.2
  42.5 0.0 copy-done.3
  42.5 0.0 copy-done.4
  42.5 0.0 copy-done.5
  42.6 0.0 copy-done.6
  42.6 0.0 copy-done.7
  42.6 0.0 copy-done.8
  42.6 0.0 copy-done.9
  42.6 9.3 %second_blur.1 = (f32[512,2048]{1,0:T(8,128)}, f32[512,2048]{1,0:T(8,128)}) custom-call(f32[512,2048]{1,0:T(8,128)S(1)} %get-tuple-element.8.now_ref, f32[64,2048]{1,0:T(8,128)S(1)} %get-tuple-element.12.edge_ref, f32[256,128]{1,0:T(8,128)S(1)} %bitcast.4, bf16[128,384]{1,0:T(8,128)(2,1)S(1)} %copy-done.8, bf16[128,384]{1,0:T(8,128)(2,1)S(1)} %copy-done.7, ...), custom_call_target="tpu_custom_call" | custom-call | flops 8000000000 | bytes 30000000 | tf_op jit(solution)/shard_map/second_blur/pallas_call | solution.py:389
Async XLA Ops:
  0.6 11.5 %copy-start.1 = (bf16[1536,256]{1,0:T(8,128)(2,1)S(1)}, bf16[1536,256]{1,0:T(8,128)(2,1)}, u32[]{:S(2)}) copy-start(bf16[1536,256]{1,0:T(8,128)(2,1)} %constant.20.clone.taps_ref) | copy-start | bytes 2359300
  0.6 11.5 %copy-start = (s32[512,2048]{1,0:T(8,128)S(1)}, s32[512,2048]{1,0:T(8,128)}, u32[]{:S(2)}) copy-start(s32[512,2048]{1,0:T(8,128)} %bottom_ref.1) | copy-start | bytes 12582916
  1.9 16.0 %collective-permute-start = (s32[32,2048]{1,0:T(8,128)S(1)}, s32[32,2048]{1,0:T(8,128)S(1)}, u32[]{:S(2)}, u32[]{:S(2)}) collective-permute-start(s32[32,2048]{1,0:T(8,128)S(1)} %get-tuple-element.9.for_odd_ref), channel_id=1, source_target_pairs={{0,0},{1,2},{2,1},{3,4},{4,3},{5,6},{6,5},{7,8},{8,7},{9,10},{10,9... | collective-permute-start | bytes 786440 | tf_op jit(solution)/shard_map/ppermute | solution.py:342
  11.9 30.6 %copy-start.2 = (bf16[256,768]{1,0:T(8,128)(2,1)S(1)}, bf16[256,768]{1,0:T(8,128)(2,1)}, u32[]{:S(2)}) copy-start(bf16[256,768]{1,0:T(8,128)(2,1)} %constant.24.clone.kerl_ref) | copy-start | bytes 1179652
  11.9 30.6 %copy-start.3 = (bf16[256,768]{1,0:T(8,128)(2,1)S(1)}, bf16[256,768]{1,0:T(8,128)(2,1)}, u32[]{:S(2)}) copy-start(bf16[256,768]{1,0:T(8,128)(2,1)} %constant.23.clone.kerh_ref) | copy-start | bytes 1179652
  11.9 30.6 %copy-start.4 = (bf16[512,256]{1,0:T(8,128)(2,1)S(1)}, bf16[512,256]{1,0:T(8,128)(2,1)}, u32[]{:S(2)}) copy-start(bf16[512,256]{1,0:T(8,128)(2,1)} %constant.19.clone.wl_ref) | copy-start | bytes 786436
  12.0 30.6 %copy-start.5 = (bf16[512,256]{1,0:T(8,128)(2,1)S(1)}, bf16[512,256]{1,0:T(8,128)(2,1)}, u32[]{:S(2)}) copy-start(bf16[512,256]{1,0:T(8,128)(2,1)} %constant.18.clone.wh_ref) | copy-start | bytes 786436
  12.0 30.6 %copy-start.6 = (bf16[448,256]{1,0:T(8,128)(2,1)S(1)}, bf16[448,256]{1,0:T(8,128)(2,1)}, u32[]{:S(2)}) copy-start(bf16[448,256]{1,0:T(8,128)(2,1)} %constant.25.clone.big_ref) | copy-start | bytes 688132
  12.0 30.6 %copy-start.7 = (bf16[128,384]{1,0:T(8,128)(2,1)S(1)}, bf16[128,384]{1,0:T(8,128)(2,1)}, u32[]{:S(2)}) copy-start(bf16[128,384]{1,0:T(8,128)(2,1)} %constant.22.clone.mixl_ref) | copy-start | bytes 294916
  12.0 30.6 %copy-start.8 = (bf16[128,384]{1,0:T(8,128)(2,1)S(1)}, bf16[128,384]{1,0:T(8,128)(2,1)}, u32[]{:S(2)}) copy-start(bf16[128,384]{1,0:T(8,128)(2,1)} %constant.21.clone.mixh_ref) | copy-start | bytes 294916
  12.0 30.6 %copy-start.9 = (bf16[128,96]{1,0:T(8,128)(2,1)S(1)}, bf16[128,96]{1,0:T(8,128)(2,1)}, u32[]{:S(2)}) copy-start(bf16[128,96]{1,0:T(8,128)(2,1)} %constant.26.clone.small_ref) | copy-start | bytes 73732
  12.0 5.9 %collective-permute-start.1 = (s32[32,2048]{1,0:T(8,128)S(1)}, s32[32,2048]{1,0:T(8,128)S(1)}, u32[]{:S(2)}, u32[]{:S(2)}) collective-permute-start(s32[32,2048]{1,0:T(8,128)S(1)} %get-tuple-element.10.for_even_ref), channel_id=1, source_target_pairs={{0,1},{1,0},{2,3},{3,2},{4,5},{5,4},{6,7},{7,6},{8,9},{9,8},{10,11... | collective-permute-start | bytes 786440 | tf_op jit(solution)/shard_map/ppermute | solution.py:343

commit v4 on v3

--- a/solution.py
+++ b/solution.py
@@ -91,8 +91,11 @@
     return kind, jnp.where(pattern == 2, 7.0, 5.0 * kind)
 
 
-LIFT = 1.05
-MIDDLE = 1.85
+def first_update(kind, forward):
+    second = kind > 1.5
+    value = jnp.maximum(1.5 * kind - forward, 0.0)
+    value = jnp.where(second, value - 1.05, value)
+    return value, jnp.where(kind > 0.5, value + jnp.where(second, 0.55, 0.5), 0.0)
 
 
 def column_sums(value):
@@ -116,7 +119,7 @@
     return packed_ref[:column], packed_ref[column : 2 * column], packed_ref[2 * column : at], packed_ref[at : at + 4 * H, : 4 * H]
 
 
-def first_kernel(pattern_ref, taps_ref, out_ref, sums_ref, rh, rl):
+def first_kernel(pattern_ref, taps_ref, out_ref, base_ref, sums_ref, rh, rl):
     wh, wl, big, small = cut(taps_ref)
     rows, width = pattern_ref.shape
     cells = width // POOL
@@ -124,8 +127,9 @@
     clear_rims(rl)
     parts = windows(H, rows - H, big.shape[1] - 2 * H)
     zeros = jnp.zeros((H, width), F32)
-    out_ref[:H] = zeros
-    out_ref[rows - H :] = zeros
+    for ref in (out_ref, base_ref):
+        ref[:H] = zeros
+        ref[rows - H :] = zeros
 
     def cell(t):
         return slice(POOL * t, POOL * (t + 1))
@@ -143,8 +147,9 @@
         window = slice(POOL * t, POOL * (t + 1) + 2 * LANES)
         forward = blur_across(rh[:, window], rl[:, window], wh, wl)
         kind, level = pixels(pattern_ref[:, cell(t)])
-        now = jnp.maximum(1.5 * kind[H : rows - H] - forward, 0.0)
+        now, base = first_update(kind[H : rows - H], forward)
         out_ref[H : rows - H, cell(t)] = now
+        base_ref[H : rows - H, cell(t)] = base
         sums = [column_sums(now[: POOL - H]), column_sums(now[POOL - H :])]
         sums += [column_sums(value[first : first + POOL]) for value in (level, kind) for first in (0, POOL)]
         sums_ref[:, cell(t)] = jnp.concatenate(sums + [jnp.zeros((2, POOL), F32)], axis=0)
@@ -156,7 +161,7 @@
             across(t - 1)
 
 
-def edge_kernel(for_odd_ref, for_even_ref, from_odd_ref, from_even_ref, sums_ref, taps_ref, edge_ref, send_ref):
+def edge_kernel(for_odd_ref, for_even_ref, from_odd_ref, from_even_ref, sums_ref, taps_ref, edge_ref, edge_base_ref, send_ref):
     count = lax.axis_size(AXES)
     me = lax.axis_index(AXES)
     width = edge_ref.shape[1]
@@ -185,14 +190,14 @@
     spread = jnp.zeros((8, LANES), F32)
     for j in range(cells):
         here = slice(POOL * j, POOL * (j + 1))
-        now = jnp.maximum(1.5 * kind[:, here] - forward[4 * H * j : 4 * H * (j + 1)], 0.0)
+        now, edge_base_ref[:, here] = first_update(kind[:, here], forward[4 * H * j : 4 * H * (j + 1)])
         edge_ref[:, here] = now
         top, bottom = column_sums(now[H : 2 * H]), column_sums(now[2 * H : 3 * H])
         sums = sums_ref[:, here] + jnp.where(row == 0, top, jnp.where(row == 1, bottom, 0.0))
         total = jnp.sum(sums, axis=1, keepdims=True)
         value, fifths, classes = total[0:2], total[2:4], total[4:6]
         second = (5.0 * classes - fifths) * (1.0 / 3.0)
-        total = jnp.concatenate([value - LIFT * second, 0.2 * fifths, classes - second, jnp.zeros((2, 1), F32)], axis=0)
+        total = jnp.concatenate([value, 0.2 * fifths, classes - second, jnp.zeros((2, 1), F32)], axis=0)
         spread = spread + jnp.where(lane == place * cells + j, total, 0.0)
     line = column_sums(spread) * (1.0 / (POOL * POOL))
     send_ref[...] = jnp.broadcast_to(line, send_ref.shape)
@@ -229,7 +234,7 @@
 
 
 def second_kernel(
-    now_ref, edge_ref, all_ref, mixh_ref, mixl_ref, kerh_ref, kerl_ref, big_ref, small_ref, wh_ref, wl_ref,
+    now_ref, base_ref, edge_ref, edge_base_ref, all_ref, mixh_ref, mixl_ref, kerh_ref, kerl_ref, big_ref, small_ref, wh_ref, wl_ref,
     dose_hbm, exposure_hbm,
     dose_ref, exposure_ref, rh, rl, up_ref, b1_ref, b2_ref, dose_sem, exposure_sem,
 ):
@@ -241,7 +246,7 @@
     def cell(t):
         return slice(POOL * t, POOL * (t + 1))
 
-    parts = windows(0, rows, wide)
+    parts = [(0, 224), (224, 416), (416, 512)]
     stores = [
         [pltpu.make_async_copy(ref.at[a:b], hbm.at[a:b], sem.at[i]) for i, (a, b) in enumerate(parts)]
         for ref, hbm, sem in ((dose_ref, dose_hbm, dose_sem), (exposure_ref, exposure_hbm, exposure_sem))
@@ -268,15 +273,15 @@
             if a >= b:
                 continue
             value = ref[at + a - start : at + b - start, cell(t)]
-            second = value > MIDDLE
-            dose = value - up_ref[line : line + 1, cell(t)]
-            dose = jnp.maximum(jnp.where(second, dose - LIFT, dose), 0.0)
-            doses.append(dose)
-            low, high = max(a, first + H), min(b, last - H)
-            if low < high:
-                base = jnp.where(dose > 0, dose + jnp.where(second, 0.55, 0.5), 0.0)
-                dose_ref[low:high, cell(t)] = base[low - a : high - a]
+            doses.append(jnp.maximum(value - up_ref[line : line + 1, cell(t)], 0.0))
         return jnp.concatenate(doses, axis=0)
+
+    own = [
+        (0, H, edge_base_ref, H, 0),
+        (H, POOL, base_ref, H, 0),
+        (POOL, rows - H, base_ref, POOL, 1),
+        (rows - H, rows, edge_base_ref, 2 * H, 1),
+    ]
 
     def across(first, last, ts):
         spans = [slice(POOL * t, POOL * (t + 1) + 2 * LANES) for t in ts]
@@ -284,19 +289,21 @@
         forward = blur_across(high, low, wh_ref[...], wl_ref[...])
         for k, t in enumerate(ts):
             here = cell(t)
-            for half in range(rows // POOL):
-                a, b = max(first, POOL * half), min(last, POOL * (half + 1))
+            for start, stop, ref, from_row, half in own:
+                a, b = max(first, start), min(last, stop)
                 if a >= b:
                     continue
                 at = k * (last - first) + a - first
-                exposure = forward[at : at + b - a] + up_ref[4 + half : 5 + half, here]
-                base = dose_ref[a:b, here]
-                exposure_ref[a:b, here] = exposure
-                dose_ref[a:b, here] = jnp.where(base > 0, base - exposure, 0.0)
+                part = forward[at : at + b - a]
+                second = up_ref[4 + half : 5 + half, here]
+                base = ref[from_row + a - start : from_row + b - start, here]
+                exposure_ref[a:b, here] = part + second
+                dose_ref[a:b, here] = jnp.where(base > 0, base - (up_ref[1 + half : 2 + half, here] + second) - part, 0.0)
 
     for i, (first, last) in enumerate(parts):
-        full = last - first == wide
-        taps = big_ref[...] if full else small_ref[...]
+        n = last - first
+        full = n > 96
+        taps = big_ref[...] if n == wide else jnp.concatenate([big_ref[:n, : n + 2 * H], big_ref[wide : wide + n, : n + 2 * H]], axis=0)
         for t in range(cells):
             here = slice(POOL * t + LANES, POOL * (t + 1) + LANES)
             part = blur_down3(taps, *split(dose_rows(first - H, last + H, t)))
@@ -348,23 +355,23 @@
     short = row_taps(2 * H, 0.2)
     short = np.concatenate([short, np.zeros((short.shape[0], POOL - short.shape[1]), short.dtype)], axis=1)
     first_taps = jnp.asarray(np.concatenate([*column_taps(1.0 / TOTAL), row_taps(wide, 0.2), short], axis=0))
-    now, sums = pl.pallas_call(
+    now, base, sums = pl.pallas_call(
         first_kernel,
         in_specs=[VMEM] * 2,
-        out_specs=[VMEM] * 2,
-        out_shape=[jax.ShapeDtypeStruct((rows, width), F32), jax.ShapeDtypeStruct((8, width), F32)],
+        out_specs=[VMEM] * 3,
+        out_shape=[jax.ShapeDtypeStruct((rows, width), F32)] * 2 + [jax.ShapeDtypeStruct((8, width), F32)],
         scratch_shapes=[pltpu.VMEM((rows - 2 * H, padded), BF16)] * 2,
-        compiler_params=params(40),
+        compiler_params=params(28),
         cost_estimate=pl.CostEstimate(flops=6 * 10**9, bytes_accessed=3 * 10**7, transcendentals=0),
         name="first_blur",
     )(pattern, first_taps)
 
-    edge, send = pl.pallas_call(
+    edge, edge_base, send = pl.pallas_call(
         edge_kernel,
         in_specs=[VMEM] * 6,
-        out_specs=[VMEM] * 2,
-        out_shape=[jax.ShapeDtypeStruct((4 * H, width), F32), jax.ShapeDtypeStruct((count, LANES), F32)],
-        compiler_params=params(40),
+        out_specs=[VMEM] * 3,
+        out_shape=[jax.ShapeDtypeStruct((4 * H, width), F32)] * 2 + [jax.ShapeDtypeStruct((count, LANES), F32)],
+        compiler_params=params(28),
         name="edge_blur",
     )(for_odd, for_even, from_odd, from_even, sums, first_taps)
 
@@ -388,7 +395,7 @@
     small = jnp.asarray(row_taps(rows % wide, 1.0))
     return pl.pallas_call(
         second_kernel,
-        in_specs=[VMEM] * 11,
+        in_specs=[VMEM] * 13,
         out_specs=[HBM] * 2,
         out_shape=[jax.ShapeDtypeStruct((rows, width), F32)] * 2,
         scratch_shapes=[pltpu.VMEM((rows, width), F32)] * 2
@@ -396,10 +403,10 @@
         + [pltpu.VMEM((8, width), F32)]
         + [pltpu.VMEM((count, LANES), F32)] * 2
         + [pltpu.SemaphoreType.DMA((cells,))] * 2,
-        compiler_params=params(44),
+        compiler_params=params(36),
         cost_estimate=pl.CostEstimate(flops=8 * 10**9, bytes_accessed=3 * 10**7, transcendentals=0),
         name="second_blur",
-    )(now, edge, gathered, *constants, big, small, taps_high, taps_low)
+    )(now, base, edge, edge_base, gathered, *constants, big, small, taps_high, taps_low)
 
 
 def solution(mesh):

time: 52.1 us -> 51.7 us (level)
  waiting for transfers between devices: 1.02 us -> 0.18 us
    ppermute x1, waiting for transfers between devices: 1.02 us -> 0.18 us  [local(): from_odd = lax.ppermute(for_odd, AXES, odd_pairs)]
  transfers between devices with their start and end apart: 2 -> 2, of which waited for: 1 -> 1; matrix products, arithmetic and copies ran while one was open for 0% -> 0% of each run, Pallas kernels for 9% -> 11%
where the time goes in v4:
time: 51.7 us; the launch traced here: 51.6 us
  blocking collectives  23.5 us (45%)
  Pallas kernels  16.7 us (32%)
  starting transfers between devices  10.1 us (20%)
  between operations  0.96 us (2%)
    all_to_all x1, blocking collectives, local(): lax.all_to_all(send.reshape(count, 1, LANES), AXES, 0, 0, tiled=True)  23.5 us
    ppermute x1, starting transfers between devices, local(): from_odd = lax.ppermute(for_odd, AXES, odd_pairs)  10 us
    pallas_call x1, Pallas kernels, local(): pl.pallas_call(second_kernel, in_specs=[VMEM] * 13, out_specs=[HBM] * 2,...  8.76 us
    pallas_call x1, Pallas kernels, local(): pl.pallas_call(first_kernel, in_specs=[VMEM] * 2, out_specs=[VMEM] * 3, o...  5.59 us
    pallas_call x1, Pallas kernels, local(): pl.pallas_call(rims_kernel, grid=(1,), in_specs=[pl.BlockSpec(strip, lamb...  1.24 us
    pallas_call x1, Pallas kernels, local(): pl.pallas_call(edge_kernel, in_specs=[VMEM] * 6, out_specs=[VMEM] * 3, ou...  1.14 us
  transfers between devices with their start and end apart: 2, of which 1 were waited for; matrix products, arithmetic and copies ran while one was open for 0% of the time, Pallas kernels for 11%

profile of v4, /device:TPU:1, one launch (start us, length us, event | category | flops | bytes accessed | tf_op | source)
XLA Modules:
  0.0 51.6 jit_solution(4923078370565402289)
XLA Ops:
  0.6 0.0 copy-start.1
  0.6 0.0 copy-start
  0.7 1.2 %rims.1 = (s32[32,2048]{1,0:T(8,128)S(1)}, s32[32,2048]{1,0:T(8,128)S(1)}) custom-call(s32[512,2048]{1,0:T(8,128)} %bottom_ref.1, s32[512,2048]{1,0:T(8,128)} %bottom_ref.1), custom_call_target="tpu_custom_call" | custom-call | tf_op jit(solution)/shard_map/rims/pallas_call | solution.py:340
  1.9 10.0 %collective-permute-start = (s32[32,2048]{1,0:T(8,128)S(1)}, s32[32,2048]{1,0:T(8,128)S(1)}, u32[]{:S(2)}, u32[]{:S(2)}) collective-permute-start(s32[32,2048]{1,0:T(8,128)S(1)} %get-tuple-element.12.for_odd_ref), channel_id=1, source_target_pairs={{0,0},{1,2},{2,1},{3,4},{4,3},{5,6},{6,5},{7,8},{8,7},{9,10},{10,9... | collective-permute-start | bytes 786440 | tf_op jit(solution)/shard_map/ppermute | solution.py:349
  11.9 0.0 copy-start.2
  11.9 0.0 copy-start.3
  11.9 0.0 copy-start.4
  12.0 0.0 copy-start.5
  12.0 0.0 copy-start.6
  12.0 0.0 copy-start.7
  12.0 0.0 copy-start.8
  12.0 0.0 copy-start.9
  12.0 0.1 collective-permute-start.1
  12.1 0.0 copy-done.1
  12.1 0.0 copy-done
  12.1 5.6 %first_blur.1 = (f32[512,2048]{1,0:T(8,128)S(1)}, f32[512,2048]{1,0:T(8,128)S(1)}, f32[8,2048]{1,0:T(8,128)S(1)}) custom-call(s32[512,2048]{1,0:T(8,128)S(1)} %copy-done, bf16[1536,256]{1,0:T(8,128)(2,1)S(1)} %copy-done.1), custom_call_target="tpu_custom_call" | custom-call | flops 6000000000 | bytes 30000000 | tf_op jit(solution)/shard_map/first_blur/pallas_call | solution.py:358
  17.7 0.2 collective-permute-done.from_odd_ref
  17.9 0.0 collective-permute-done.1.from_even_ref
  17.9 1.1 %edge_blur.1 = (f32[64,2048]{1,0:T(8,128)S(1)}, f32[64,2048]{1,0:T(8,128)S(1)}, f32[256,128]{1,0:T(8,128)S(1)}) custom-call(s32[32,2048]{1,0:T(8,128)S(1)} %get-tuple-element.12.for_odd_ref, s32[32,2048]{1,0:T(8,128)S(1)} %get-tuple-element.13.for_even_ref, s32[32,2048]{1,0:T(8,128)S(1)} %collective-permute-done.from_odd_ref, ...), custom_call_target="tpu_custom_call" | custom-call | tf_op jit(solution)/shard_map/edge_blur/pallas_call | solution.py:369
  19.1 23.5 %all_to_all.5 = f32[256,1,128]{2,1,0:T(1,128)S(1)} all-to-all(f32[256,1,128]{2,1,0:T(1,128)S(1)} %bitcast.5), channel_id=1, replica_groups=mesh['band'=16,'strip'=16] {'band','strip'}, dimensions={0} | all-to-all | bytes 262144 | tf_op jit(solution)/shard_map/all_to_all | solution.py:378
  42.6 0.0 copy-done.2
  42.6 0.0 copy-done.3
  42.6 0.0 copy-done.4
  42.6 0.0 copy-done.5
  42.6 0.0 copy-done.6
  42.6 0.0 copy-done.7
  42.7 0.0 copy-done.8
  42.7 0.0 copy-done.9
  42.7 8.8 %second_blur.1 = (f32[512,2048]{1,0:T(8,128)}, f32[512,2048]{1,0:T(8,128)}) custom-call(f32[512,2048]{1,0:T(8,128)S(1)} %get-tuple-element.10.now_ref, f32[512,2048]{1,0:T(8,128)S(1)} %get-tuple-element.11.base_ref, f32[64,2048]{1,0:T(8,128)S(1)} %get-tuple-element.15.edge_ref, f32[64,2048]{1,0:T(8,128)S(1)} %get-tuple-element.16.edge_base_ref, ...), custom_call_target="tpu_custom_call" | custom-call | flops 8000000000 | bytes 30000000 | tf_op jit(solution)/shard_map/second_blur/pallas_call | solution.py:396
Async XLA Ops:
  0.6 11.5 %copy-start.1 = (bf16[1536,256]{1,0:T(8,128)(2,1)S(1)}, bf16[1536,256]{1,0:T(8,128)(2,1)}, u32[]{:S(2)}) copy-start(bf16[1536,256]{1,0:T(8,128)(2,1)} %constant.20.clone.taps_ref) | copy-start | bytes 2359300
  0.6 11.5 %copy-start = (s32[512,2048]{1,0:T(8,128)S(1)}, s32[512,2048]{1,0:T(8,128)}, u32[]{:S(2)}) copy-start(s32[512,2048]{1,0:T(8,128)} %bottom_ref.1) | copy-start | bytes 12582916
  1.9 16.0 %collective-permute-start = (s32[32,2048]{1,0:T(8,128)S(1)}, s32[32,2048]{1,0:T(8,128)S(1)}, u32[]{:S(2)}, u32[]{:S(2)}) collective-permute-start(s32[32,2048]{1,0:T(8,128)S(1)} %get-tuple-element.12.for_odd_ref), channel_id=1, source_target_pairs={{0,0},{1,2},{2,1},{3,4},{4,3},{5,6},{6,5},{7,8},{8,7},{9,10},{10,9... | collective-permute-start | bytes 786440 | tf_op jit(solution)/shard_map/ppermute | solution.py:349
  11.9 30.7 %copy-start.2 = (bf16[256,768]{1,0:T(8,128)(2,1)S(1)}, bf16[256,768]{1,0:T(8,128)(2,1)}, u32[]{:S(2)}) copy-start(bf16[256,768]{1,0:T(8,128)(2,1)} %constant.24.clone.kerl_ref) | copy-start | bytes 1179652
  11.9 30.7 %copy-start.3 = (bf16[256,768]{1,0:T(8,128)(2,1)S(1)}, bf16[256,768]{1,0:T(8,128)(2,1)}, u32[]{:S(2)}) copy-start(bf16[256,768]{1,0:T(8,128)(2,1)} %constant.23.clone.kerh_ref) | copy-start | bytes 1179652
  11.9 30.7 %copy-start.4 = (bf16[512,256]{1,0:T(8,128)(2,1)S(1)}, bf16[512,256]{1,0:T(8,128)(2,1)}, u32[]{:S(2)}) copy-start(bf16[512,256]{1,0:T(8,128)(2,1)} %constant.19.clone.wl_ref) | copy-start | bytes 786436
  12.0 30.7 %copy-start.5 = (bf16[512,256]{1,0:T(8,128)(2,1)S(1)}, bf16[512,256]{1,0:T(8,128)(2,1)}, u32[]{:S(2)}) copy-start(bf16[512,256]{1,0:T(8,128)(2,1)} %constant.18.clone.wh_ref) | copy-start | bytes 786436
  12.0 30.7 %copy-start.6 = (bf16[448,256]{1,0:T(8,128)(2,1)S(1)}, bf16[448,256]{1,0:T(8,128)(2,1)}, u32[]{:S(2)}) copy-start(bf16[448,256]{1,0:T(8,128)(2,1)} %constant.25.clone.big_ref) | copy-start | bytes 688132
  12.0 30.7 %copy-start.7 = (bf16[128,384]{1,0:T(8,128)(2,1)S(1)}, bf16[128,384]{1,0:T(8,128)(2,1)}, u32[]{:S(2)}) copy-start(bf16[128,384]{1,0:T(8,128)(2,1)} %constant.22.clone.mixl_ref) | copy-start | bytes 294916
  12.0 30.7 %copy-start.8 = (bf16[128,384]{1,0:T(8,128)(2,1)S(1)}, bf16[128,384]{1,0:T(8,128)(2,1)}, u32[]{:S(2)}) copy-start(bf16[128,384]{1,0:T(8,128)(2,1)} %constant.21.clone.mixh_ref) | copy-start | bytes 294916
  12.0 30.7 %copy-start.9 = (bf16[128,96]{1,0:T(8,128)(2,1)S(1)}, bf16[128,96]{1,0:T(8,128)(2,1)}, u32[]{:S(2)}) copy-start(bf16[128,96]{1,0:T(8,128)(2,1)} %constant.26.clone.small_ref) | copy-start | bytes 73732
  12.0 5.9 %collective-permute-start.1 = (s32[32,2048]{1,0:T(8,128)S(1)}, s32[32,2048]{1,0:T(8,128)S(1)}, u32[]{:S(2)}, u32[]{:S(2)}) collective-permute-start(s32[32,2048]{1,0:T(8,128)S(1)} %get-tuple-element.13.for_even_ref), channel_id=1, source_target_pairs={{0,1},{1,0},{2,3},{3,2},{4,5},{5,4},{6,7},{7,6},{8,9},{9,8},{10,11... | collective-permute-start | bytes 786440 | tf_op jit(solution)/shard_map/ppermute | solution.py:350

commit v5 on v4

--- a/solution.py
+++ b/solution.py
@@ -154,11 +154,11 @@
         sums += [column_sums(value[first : first + POOL]) for value in (level, kind) for first in (0, POOL)]
         sums_ref[:, cell(t)] = jnp.concatenate(sums + [jnp.zeros((2, POOL), F32)], axis=0)
 
-    for t in range(cells + 1):
+    for t in range(cells + 2):
         if t < cells:
             down(t)
-        if t > 0:
-            across(t - 1)
+        if t > 1:
+            across(t - 2)
 
 
 def edge_kernel(for_odd_ref, for_even_ref, from_odd_ref, from_even_ref, sums_ref, taps_ref, edge_ref, edge_base_ref, send_ref):
@@ -308,9 +308,10 @@
             here = slice(POOL * t + LANES, POOL * (t + 1) + LANES)
             part = blur_down3(taps, *split(dose_rows(first - H, last + H, t)))
             rh[first:last, here], rl[first:last, here] = split(part)
-            if full and t > 0:
-                across(first, last, [t - 1])
-        across(first, last, [cells - 1] if full else list(range(cells)))
+            if full and t > 1:
+                across(first, last, [t - 2])
+        for group in [[cells - 2], [cells - 1]] if full else [list(range(cells))]:
+            across(first, last, group)
         for group in stores:
             group[i].start()
     for group in stores:

time: 51.7 us -> 51.4 us (level)
  transfers between devices with their start and end apart: 2 -> 2, of which waited for: 1 -> 0; matrix products, arithmetic and copies ran while one was open for 0% -> 0% of each run, Pallas kernels for 11% -> 11%
where the time goes in v5:
time: 51.4 us; the launch traced here: 51.3 us
  blocking collectives  23.4 us (46%)
  Pallas kernels  16.7 us (32%)
  starting transfers between devices  10.1 us (20%)
  between operations  0.98 us (2%)
    all_to_all x1, blocking collectives, local(): lax.all_to_all(send.reshape(count, 1, LANES), AXES, 0, 0, tiled=True)  23.4 us
    ppermute x1, starting transfers between devices, local(): from_odd = lax.ppermute(for_odd, AXES, odd_pairs)  10 us
    pallas_call x1, Pallas kernels, local(): pl.pallas_call(second_kernel, in_specs=[VMEM] * 13, out_specs=[HBM] * 2,...  8.48 us
    pallas_call x1, Pallas kernels, local(): pl.pallas_call(first_kernel, in_specs=[VMEM] * 2, out_specs=[VMEM] * 3, o...  5.84 us
    pallas_call x1, Pallas kernels, local(): pl.pallas_call(rims_kernel, grid=(1,), in_specs=[pl.BlockSpec(strip, lamb...  1.24 us
    pallas_call x1, Pallas kernels, local(): pl.pallas_call(edge_kernel, in_specs=[VMEM] * 6, out_specs=[VMEM] * 3, ou...  1.15 us
  transfers between devices with their start and end apart: 2, of which 0 were waited for; matrix products, arithmetic and copies ran while one was open for 0% of the time, Pallas kernels for 11%

profile of v5, /device:TPU:1, one launch (start us, length us, event | category | flops | bytes accessed | tf_op | source)
XLA Modules:
  0.0 51.3 jit_solution(8062198382686352054)
XLA Ops:
  0.6 0.0 copy-start.1
  0.6 0.0 copy-start
  0.7 1.2 %rims.1 = (s32[32,2048]{1,0:T(8,128)S(1)}, s32[32,2048]{1,0:T(8,128)S(1)}) custom-call(s32[512,2048]{1,0:T(8,128)} %bottom_ref.1, s32[512,2048]{1,0:T(8,128)} %bottom_ref.1), custom_call_target="tpu_custom_call" | custom-call | tf_op jit(solution)/shard_map/rims/pallas_call | solution.py:341
  1.9 10.0 %collective-permute-start = (s32[32,2048]{1,0:T(8,128)S(1)}, s32[32,2048]{1,0:T(8,128)S(1)}, u32[]{:S(2)}, u32[]{:S(2)}) collective-permute-start(s32[32,2048]{1,0:T(8,128)S(1)} %get-tuple-element.12.for_odd_ref), channel_id=1, source_target_pairs={{0,0},{1,2},{2,1},{3,4},{4,3},{5,6},{6,5},{7,8},{8,7},{9,10},{10,9... | collective-permute-start | bytes 786440 | tf_op jit(solution)/shard_map/ppermute | solution.py:350
  11.9 0.0 copy-start.2
  11.9 0.0 copy-start.3
  11.9 0.0 copy-start.4
  12.0 0.0 copy-start.5
  12.0 0.0 copy-start.6
  12.0 0.0 copy-start.7
  12.0 0.0 copy-start.8
  12.0 0.0 copy-start.9
  12.0 0.1 collective-permute-start.1
  12.1 0.0 copy-done.1
  12.1 0.0 copy-done
  12.1 5.8 %first_blur.1 = (f32[512,2048]{1,0:T(8,128)S(1)}, f32[512,2048]{1,0:T(8,128)S(1)}, f32[8,2048]{1,0:T(8,128)S(1)}) custom-call(s32[512,2048]{1,0:T(8,128)S(1)} %copy-done, bf16[1536,256]{1,0:T(8,128)(2,1)S(1)} %copy-done.1), custom_call_target="tpu_custom_call" | custom-call | flops 6000000000 | bytes 30000000 | tf_op jit(solution)/shard_map/first_blur/pallas_call | solution.py:359
  18.0 0.0 collective-permute-done.from_odd_ref
  18.0 0.0 collective-permute-done.1.from_even_ref
  18.0 1.1 %edge_blur.1 = (f32[64,2048]{1,0:T(8,128)S(1)}, f32[64,2048]{1,0:T(8,128)S(1)}, f32[256,128]{1,0:T(8,128)S(1)}) custom-call(s32[32,2048]{1,0:T(8,128)S(1)} %get-tuple-element.12.for_odd_ref, s32[32,2048]{1,0:T(8,128)S(1)} %get-tuple-element.13.for_even_ref, s32[32,2048]{1,0:T(8,128)S(1)} %collective-permute-done.from_odd_ref, ...), custom_call_target="tpu_custom_call" | custom-call | tf_op jit(solution)/shard_map/edge_blur/pallas_call | solution.py:370
  19.2 23.4 %all_to_all.5 = f32[256,1,128]{2,1,0:T(1,128)S(1)} all-to-all(f32[256,1,128]{2,1,0:T(1,128)S(1)} %bitcast.5), channel_id=1, replica_groups=mesh['band'=16,'strip'=16] {'band','strip'}, dimensions={0} | all-to-all | bytes 262144 | tf_op jit(solution)/shard_map/all_to_all | solution.py:379
  42.6 0.0 copy-done.2
  42.6 0.0 copy-done.3
  42.6 0.0 copy-done.4
  42.6 0.0 copy-done.5
  42.6 0.0 copy-done.6
  42.6 0.0 copy-done.7
  42.7 0.0 copy-done.8
  42.7 0.0 copy-done.9
  42.7 8.5 %second_blur.1 = (f32[512,2048]{1,0:T(8,128)}, f32[512,2048]{1,0:T(8,128)}) custom-call(f32[512,2048]{1,0:T(8,128)S(1)} %get-tuple-element.10.now_ref, f32[512,2048]{1,0:T(8,128)S(1)} %get-tuple-element.11.base_ref, f32[64,2048]{1,0:T(8,128)S(1)} %get-tuple-element.15.edge_ref, f32[64,2048]{1,0:T(8,128)S(1)} %get-tuple-element.16.edge_base_ref, ...), custom_call_target="tpu_custom_call" | custom-call | flops 8000000000 | bytes 30000000 | tf_op jit(solution)/shard_map/second_blur/pallas_call | solution.py:397
Async XLA Ops:
  0.6 11.5 %copy-start.1 = (bf16[1536,256]{1,0:T(8,128)(2,1)S(1)}, bf16[1536,256]{1,0:T(8,128)(2,1)}, u32[]{:S(2)}) copy-start(bf16[1536,256]{1,0:T(8,128)(2,1)} %constant.20.clone.taps_ref) | copy-start | bytes 2359300
  0.6 11.5 %copy-start = (s32[512,2048]{1,0:T(8,128)S(1)}, s32[512,2048]{1,0:T(8,128)}, u32[]{:S(2)}) copy-start(s32[512,2048]{1,0:T(8,128)} %bottom_ref.1) | copy-start | bytes 12582916
  1.9 16.1 %collective-permute-start = (s32[32,2048]{1,0:T(8,128)S(1)}, s32[32,2048]{1,0:T(8,128)S(1)}, u32[]{:S(2)}, u32[]{:S(2)}) collective-permute-start(s32[32,2048]{1,0:T(8,128)S(1)} %get-tuple-element.12.for_odd_ref), channel_id=1, source_target_pairs={{0,0},{1,2},{2,1},{3,4},{4,3},{5,6},{6,5},{7,8},{8,7},{9,10},{10,9... | collective-permute-start | bytes 786440 | tf_op jit(solution)/shard_map/ppermute | solution.py:350
  11.9 30.7 %copy-start.2 = (bf16[256,768]{1,0:T(8,128)(2,1)S(1)}, bf16[256,768]{1,0:T(8,128)(2,1)}, u32[]{:S(2)}) copy-start(bf16[256,768]{1,0:T(8,128)(2,1)} %constant.24.clone.kerl_ref) | copy-start | bytes 1179652
  11.9 30.7 %copy-start.3 = (bf16[256,768]{1,0:T(8,128)(2,1)S(1)}, bf16[256,768]{1,0:T(8,128)(2,1)}, u32[]{:S(2)}) copy-start(bf16[256,768]{1,0:T(8,128)(2,1)} %constant.23.clone.kerh_ref) | copy-start | bytes 1179652
  11.9 30.7 %copy-start.4 = (bf16[512,256]{1,0:T(8,128)(2,1)S(1)}, bf16[512,256]{1,0:T(8,128)(2,1)}, u32[]{:S(2)}) copy-start(bf16[512,256]{1,0:T(8,128)(2,1)} %constant.19.clone.wl_ref) | copy-start | bytes 786436
  12.0 30.7 %copy-start.5 = (bf16[512,256]{1,0:T(8,128)(2,1)S(1)}, bf16[512,256]{1,0:T(8,128)(2,1)}, u32[]{:S(2)}) copy-start(bf16[512,256]{1,0:T(8,128)(2,1)} %constant.18.clone.wh_ref) | copy-start | bytes 786436
  12.0 30.7 %copy-start.6 = (bf16[448,256]{1,0:T(8,128)(2,1)S(1)}, bf16[448,256]{1,0:T(8,128)(2,1)}, u32[]{:S(2)}) copy-start(bf16[448,256]{1,0:T(8,128)(2,1)} %constant.25.clone.big_ref) | copy-start | bytes 688132
  12.0 30.7 %copy-start.7 = (bf16[128,384]{1,0:T(8,128)(2,1)S(1)}, bf16[128,384]{1,0:T(8,128)(2,1)}, u32[]{:S(2)}) copy-start(bf16[128,384]{1,0:T(8,128)(2,1)} %constant.22.clone.mixl_ref) | copy-start | bytes 294916
  12.0 30.7 %copy-start.8 = (bf16[128,384]{1,0:T(8,128)(2,1)S(1)}, bf16[128,384]{1,0:T(8,128)(2,1)}, u32[]{:S(2)}) copy-start(bf16[128,384]{1,0:T(8,128)(2,1)} %constant.21.clone.mixh_ref) | copy-start | bytes 294916
  12.0 30.7 %copy-start.9 = (bf16[128,96]{1,0:T(8,128)(2,1)S(1)}, bf16[128,96]{1,0:T(8,128)(2,1)}, u32[]{:S(2)}) copy-start(bf16[128,96]{1,0:T(8,128)(2,1)} %constant.26.clone.small_ref) | copy-start | bytes 73732
  12.0 6.0 %collective-permute-start.1 = (s32[32,2048]{1,0:T(8,128)S(1)}, s32[32,2048]{1,0:T(8,128)S(1)}, u32[]{:S(2)}, u32[]{:S(2)}) collective-permute-start(s32[32,2048]{1,0:T(8,128)S(1)} %get-tuple-element.13.for_even_ref), channel_id=1, source_target_pairs={{0,1},{1,0},{2,3},{3,2},{4,5},{5,4},{6,7},{7,6},{8,9},{9,8},{10,11... | collective-permute-start | bytes 786440 | tf_op jit(solution)/shard_map/ppermute | solution.py:351
